TPU v7x, 512 devices: a whole 4x4x16 slice. The times are simulated.
512 devices in a mesh: fsdp: 32 (over x_lo, z), side: 16 (over y, x_hi, core).
Axes of the slice: x: 4 (x_hi: 2, x_lo: 2; x = x_hi * 2 + x_lo), y: 4, z: 16, core: 2. Of those that a mesh axis runs over, the one named last changes fastest.
Arguments:
- attn_inputs: bfloat16 [65536, 5120], P(('side', 'fsdp')), may hold values from -24 to 24
- queries: bfloat16 [65536, 2560], P(('side', 'fsdp')), may hold values from -310 to 310
- key_vectors: bfloat16 [65536, 512], P(('side', 'fsdp')), may hold values from -12 to 12
- logp_grad: bfloat16 [65536, 2560], P(('side', 'fsdp')), may hold values from -24 to 24
- new_logp: float32 [65536], P(('side', 'fsdp')), may hold values from -6.5 to -0.01
- old_logp: float32 [65536], P(('side', 'fsdp')), may hold values from -4 to -0.05
- rewards: float32 [32], replicated, may hold values from -8 to 8
- group_ids: int32 [32], replicated, may hold values from 0 to 7
- lengths: int32 [32], replicated, may hold values from 1024 to 2048
- value_proj: bfloat16 [5120, 512], P('fsdp'), may hold values from -0.078125 to 0.078125
- first_moment: bfloat16 [5120, 512], P(('fsdp', 'side')), may hold values from -120 to 120
- second_moment: bfloat16 [5120, 512], P(('fsdp', 'side')), may hold values from 100 to 9984
Outputs:
- input_grad: bfloat16 [65536, 5120], P(('side', 'fsdp'))
- new_proj: bfloat16 [5120, 512], P('fsdp')
- new_first: bfloat16 [5120, 512], P(('fsdp', 'side'))
- new_second: bfloat16 [5120, 512], P(('fsdp', 'side'))
All inputs are finite; a program needn't handle non-finite values.
Results may differ from a plain program's by a relative error of at most 0.03.
Values may be sent and summed in bfloat16 or wider, within the bound.
A program may use at most 64 MiB of HBM per device.

v0:
```python
import math

import jax
import jax.numpy as jnp
from jax import lax
from jax.sharding import Mesh
from jax.sharding import PartitionSpec as P

QH = 20
KVH = 4
HEAD = 128
ROLLS = 2
FSDP = ("fsdp_0", "fsdp_1")
SIDE_FSDP = ("side", "fsdp_0", "fsdp_1")
FSDP_SIDE = ("fsdp_0", "fsdp_1", "side")


clip_low = 0.8
clip_high = 1.2
decay_first = 0.9
decay_second = 0.95
step_rate = 0.001
weight_decay = 0.1
adam_eps = 1e-08
bias_first = 1.0 - 0.9**10
bias_second = 1.0 - 0.95**10


def laid_out(pieces, dim):
    pieces = jnp.moveaxis(pieces, 0, dim)
    dims = pieces.shape
    return pieces.reshape(*dims[:dim], dims[dim] * dims[dim + 1], *dims[dim + 2 :])


def all_blocks(value, axes, sequence):
    pieces = value
    for k in sequence:
        pieces = lax.all_gather(pieces, axes[k])
    done = sequence[::-1]
    back = [done.index(k) for k in range(len(axes))]
    pieces = pieces.transpose(*back, *range(len(axes), pieces.ndim))
    return pieces.reshape(-1, *value.shape)


def whole_of(value, axes, sequence, dim):
    return laid_out(all_blocks(value, axes, sequence), dim)


def reduced_to_own(pieces, axes, sequence):
    dims = [lax.axis_size(a) for a in axes]
    pieces = pieces.reshape(*dims, *pieces.shape[1:])
    pieces = pieces.transpose(*sequence, *range(len(axes), pieces.ndim))
    pieces = pieces.reshape(-1, *pieces.shape[len(axes) :])
    for k in sequence:
        pieces = lax.psum_scatter(pieces, axes[k], scatter_dimension=0, tiled=True)
    return pieces[0]


def split_up(value, dim, peers):
    before, after = (value.shape[:dim], value.shape[dim + 1 :])
    return jnp.moveaxis(value.reshape(*before, peers, -1, *after), dim, 0)


def summed_rows(value, axes, sequence, dim):
    peers = lax.axis_size(axes)
    return reduced_to_own(split_up(value, dim, peers), axes, sequence)


def sum_at_owner(value, axis, dim):
    pieces = split_up(value, dim, lax.axis_size(axis))
    arrived = lax.all_to_all(pieces, axis, split_axis=0, concat_axis=0, tiled=True)
    return arrived.astype(jnp.float32).sum(axis=0)


def from_everyone(value, axis):
    peers = lax.axis_size(axis)
    return lax.all_to_all(
        jnp.broadcast_to(value[None], (peers, *value.shape)), axis, 0, 0, tiled=True
    )


def collect(value, axis, dim):
    pieces = from_everyone(value, axis)
    return laid_out(pieces, dim)


def advantages(rewards, group_ids):
    group_count = rewards.shape[0] // 4
    member = (group_ids[:, None] == jnp.arange(group_count, dtype=jnp.int32)[None, :]).astype(
        jnp.float32
    )
    counts = jnp.maximum(jnp.sum(member, axis=0), 1.0)
    group_mean = jnp.sum(member * rewards[:, None], axis=0) / counts
    own_mean = jnp.sum(member * group_mean[None, :], axis=1)
    spread = rewards - own_mean
    variance = jnp.sum(member * (spread * spread)[:, None], axis=0) / counts
    own_std = jnp.sqrt(jnp.sum(member * variance[None, :], axis=1))
    return spread / jnp.maximum(own_std, 1.0)


def coefficient(new_lp, old_lp, adv_tok, len_tok, pos_tok, full_len):
    ratio_now = jnp.exp(new_lp - old_lp)
    clipped = jnp.clip(ratio_now, clip_low, clip_high)
    active = (ratio_now * adv_tok <= clipped * adv_tok) & (pos_tok < len_tok)
    len_weight = full_len / len_tok.astype(jnp.float32)
    return jnp.where(active, -adv_tok * ratio_now * len_weight, 0.0)


def block_values(query_blk, grad_blk, roll_keys, first_pos):
    tok_rows = query_blk.shape[0]
    key_count = roll_keys.shape[0]
    per_group = QH // KVH
    score_scale = 1.0 / math.sqrt(HEAD)
    query_pos = first_pos + jnp.arange(tok_rows, dtype=jnp.int32)
    key_pos = jnp.arange(key_count, dtype=jnp.int32)
    allowed = jnp.tile(key_pos[None, :] <= query_pos[:, None], (per_group, 1))
    pieces = []
    for kv_head in range(KVH):
        col_low = kv_head * per_group * HEAD
        col_high = col_low + per_group * HEAD
        q_part = (
            query_blk[:, col_low:col_high]
            .reshape(tok_rows, per_group, HEAD)
            .transpose(1, 0, 2)
            .reshape(per_group * tok_rows, HEAD)
        )
        g_part = (
            grad_blk[:, col_low:col_high]
            .reshape(tok_rows, per_group, HEAD)
            .transpose(1, 0, 2)
            .reshape(per_group * tok_rows, HEAD)
        )
        k_part = roll_keys[:, kv_head * HEAD : (kv_head + 1) * HEAD]
        scores = jnp.dot(q_part, k_part.T, preferred_element_type=jnp.float32) * score_scale
        scores = jnp.where(allowed, scores, -1e30)
        top_val = jnp.max(scores, axis=1, keepdims=True)
        expo = jnp.exp(scores - top_val)
        attention = (expo / jnp.sum(expo, axis=1, keepdims=True)).astype(jnp.bfloat16)
        pieces.append(jnp.dot(attention.T, g_part, preferred_element_type=jnp.float32))
    return jnp.concatenate(pieces, axis=1)


def adam_rows(old_rows, grad_rows, first_moment, second_moment):
    first = decay_first * first_moment.astype(jnp.float32) + (1.0 - decay_first) * grad_rows
    second = (
        decay_second * second_moment.astype(jnp.float32)
        + (1.0 - decay_second) * grad_rows * grad_rows
    )
    weight_now = old_rows.astype(jnp.float32)
    update = (
        first / bias_first / (jnp.sqrt(second / bias_second) + adam_eps) + weight_decay * weight_now
    )
    return (
        (weight_now - step_rate * update).astype(jnp.bfloat16),
        first.astype(jnp.bfloat16),
        second.astype(jnp.bfloat16),
    )


def shards(
    attn_inputs,
    queries,
    key_vectors,
    logp_grad,
    new_logp,
    old_logp,
    rewards,
    group_ids,
    lengths,
    value_proj,
    first_moment,
    second_moment,
):
    fsdp_size = lax.axis_size(FSDP)
    fsdp_index = lax.axis_index(FSDP)
    side_index = lax.axis_index("side")
    tok_rows = attn_inputs.shape[0]
    half = tok_rows // ROLLS
    full_len = half * fsdp_size
    width = key_vectors.shape[1]
    first_pos = fsdp_index * half
    advantage = advantages(rewards, group_ids)
    slot = jnp.arange(tok_rows, dtype=jnp.int32)
    global_roll = side_index * ROLLS + slot // half
    position = first_pos + slot % half
    coeff = coefficient(
        new_logp, old_logp, advantage[global_roll], lengths[global_roll], position, full_len
    )
    out_grad = (coeff[:, None] * logp_grad.astype(jnp.float32)).astype(jnp.bfloat16)
    in_columns = lax.all_to_all(attn_inputs, FSDP, split_axis=1, concat_axis=0, tiled=True)
    all_keys = whole_of(key_vectors, FSDP, (0, 1), 0)
    keys_split = all_keys.reshape(fsdp_size, ROLLS, half, width)
    partials = []
    for roll in range(ROLLS):
        roll_keys = keys_split[:, roll].reshape(full_len, width)
        partials.append(
            block_values(
                queries[roll * half : (roll + 1) * half],
                out_grad[roll * half : (roll + 1) * half],
                roll_keys,
                first_pos,
            )
        )
    stacked = jnp.stack(partials, axis=0)
    placed = (
        stacked.reshape(ROLLS, fsdp_size, half, width)
        .transpose(1, 0, 2, 3)
        .reshape(fsdp_size * tok_rows, width)
    )
    own_grad = (
        summed_rows(placed.astype(jnp.bfloat16), FSDP, (1, 0), 0)
        .astype(jnp.float32)
        .astype(jnp.bfloat16)
    )
    values_grad = lax.all_gather(own_grad, FSDP, axis=0, tiled=True)
    grad_cols = jnp.dot(values_grad, value_proj.T, preferred_element_type=jnp.float32).astype(
        jnp.bfloat16
    )
    input_grad = lax.all_to_all(grad_cols, FSDP, split_axis=0, concat_axis=1, tiled=True)
    weight_grad = lax.dot_general(
        in_columns, values_grad, (((0,), (0,)), ((), ())), preferred_element_type=jnp.float32
    )
    shard_grad = sum_at_owner(weight_grad.astype(jnp.bfloat16), "side", 0)
    shard_rows = shard_grad.shape[0]
    old_rows = lax.dynamic_slice_in_dim(value_proj, side_index * shard_rows, shard_rows, 0)
    new_rows, new_first, new_second = adam_rows(old_rows, shard_grad, first_moment, second_moment)
    new_proj = collect(new_rows, "side", 0)
    return (input_grad, new_proj, new_first, new_second)


def solution(mesh):
    torus = Mesh(mesh.devices.reshape(2, 16, mesh.shape["side"]), ("fsdp_0", "fsdp_1", "side"))
    placed = (
        P(SIDE_FSDP, None),
        P(SIDE_FSDP, None),
        P(SIDE_FSDP, None),
        P(SIDE_FSDP, None),
        P(SIDE_FSDP),
        P(SIDE_FSDP),
        P(),
        P(),
        P(),
        P(FSDP, None),
        P(FSDP_SIDE, None),
        P(FSDP_SIDE, None),
    )
    return jax.shard_map(
        shards,
        mesh=torus,
        in_specs=placed,
        out_specs=(P(SIDE_FSDP, None), P(FSDP, None), P(FSDP_SIDE, None), P(FSDP_SIDE, None)),
        check_vma=False,
    )
```

profile of v0, /device:TPU:33, one launch (start us, length us, event | category | flops | bytes accessed | tf_op | source)
XLA Modules:
  0.0 513.9 jit_solution(6397335464819392959)
XLA Ops:
  7.3 7.1 %all-gather = bf16[256,512]{1,0:T(8,128)(2,1)} all-gather(bf16[128,512]{1,0:T(8,128)(2,1)} %param.14), channel_id=2, replica_groups=mesh['fsdp_0'=2,'fsdp_1'=16,'side'=16] {'fsdp_0'}, dimensions={0}, use_global_device_ids=true | all-gather | bytes 393216 | tf_op jit(solution)/shard_map/all_gather | solution.py:38
  14.4 1.2 fusion.53
  15.8 0.8 convert_reduce_fusion.1
  16.7 0.7 select_reduce_fusion.2
  18.1 0.8 select_reduce_fusion.1
  18.8 0.7 select_reduce_fusion
  19.6 1.2 gather_fusion
  20.9 1.2 gather_fusion.1
  29.6 58.6 %all-gather.6.cloned.1.call-done = bf16[32,128,512]{2,1,0:T(8,128)(2,1)} async-done(((bf16[2,128,512]{2,1,0:T(8,128)(2,1)}), bf16[32,128,512]{2,1,0:T(8,128)(2,1)}) %all-gather.6.cloned.1.call-update) | async-done | bytes 4194320 | tf_op jit(solution)/shard_map/all_gather | solution.py:38
  88.2 2.6 copy.92
  94.8 0.7 convolution_convert_fusion.8
  100.5 1.5 pad_maximum_fusion
  101.9 3.9 copy.100
  115.1 2.6 copy.109
  117.7 2.6 maximum_bitcast_fusion
  120.8 2.4 copy.111
  123.3 75.0 %reduce-scatter.3.cloned.1.call-done = bf16[2,128,512]{2,1,0:T(8,128)(2,1)} async-done(((bf16[32,128,512]{2,1,0:T(8,128)(2,1)}), bf16[2,128,512]{2,1,0:T(8,128)(2,1)}) %reduce-scatter.3.cloned.1.call-update) | async-done | bytes 262160 | tf_op jit(solution)/shard_map/reduce_scatter | solution.py:55
  198.3 33.3 %reduce-scatter.5.cloned.1.call-done = bf16[1,128,512]{2,1,0:T(8,128)(2,1)} async-done(((bf16[2,128,512]{2,1,0:T(8,128)(2,1)}), bf16[1,128,512]{2,1,0:T(8,128)(2,1)}) %reduce-scatter.5.cloned.1.call-update) | async-done | bytes 131088 | tf_op jit(solution)/shard_map/reduce_scatter | solution.py:55
  231.6 0.8 copy.113
  232.4 89.5 %all_to_all.48 = bf16[128,32,160]{0,2,1:T(8,128)(2,1)S(1)} all-to-all(bf16[128,32,160]{0,2,1:T(8,128)(2,1)S(1)} %bitcast.123), channel_id=1, replica_groups=mesh['fsdp_0'=2,'fsdp_1'=16,'side'=16] {'fsdp_0','fsdp_1'}, dimensions={1} | all-to-all | bytes 2621440 | tf_op jit(solution)/shard_map/all_to_all | solution.py:190
  321.9 65.4 %all-gather.8.cloned.1.call-done = bf16[1,4096,512]{2,1,0:T(8,128)(2,1)} async-done(((bf16[1,128,512]{2,1,0:T(8,128)(2,1)}), bf16[1,4096,512]{2,1,0:T(8,128)(2,1)}) %all-gather.8.cloned.1.call-update) | async-done | bytes 4194320 | tf_op jit(solution)/shard_map/all_gather | solution.py:215
  387.4 3.0 fusion.29
  390.4 0.8 reshape.265
  391.2 20.8 %all-to-all-start.2 = ((bf16[16,10,512]{2,1,0:T(8,128)(2,1)}), bf16[16,10,512]{2,1,0:T(8,128)(2,1)S(1)}, u32[]{:S(2)}, u32[]{:S(2)}) async-start(bf16[16,10,512]{2,1,0:T(8,128)(2,1)} %reshape.265), calls=%async_computation.4 | async-start | bytes 524288 | tf_op jit(solution)/shard_map/all_to_all | solution.py:71
  412.0 8.7 %all-to-all-done.2 = bf16[16,10,512]{2,1,0:T(8,128)(2,1)S(1)} async-done(((bf16[16,10,512]{2,1,0:T(8,128)(2,1)}), bf16[16,10,512]{2,1,0:T(8,128)(2,1)S(1)}, u32[]{:S(2)}, u32[]{:S(2)}) %all-to-all-start.2) | async-done | bytes 163872 | tf_op jit(solution)/shard_map/all_to_all | solution.py:71
  422.1 4.3 all-to-all-start.3
  426.4 3.7 fusion.19
  430.1 1.3 copy.127
  431.4 3.7 all-to-all-done.3
  435.1 5.5 %all-to-all-start = ((bf16[32,128,160]{1,2,0:T(8,128)(2,1)}), bf16[32,128,160]{1,2,0:T(8,128)(2,1)S(1)}, u32[]{:S(2)}, u32[]{:S(2)}) async-start(bf16[32,128,160]{1,2,0:T(8,128)(2,1)} %bitcast.100), calls=%async_computation.2 | async-start | bytes 2621440 | tf_op jit(solution)/shard_map/all_to_all | solution.py:219
  441.4 64.5 %all-to-all-done = bf16[32,128,160]{1,2,0:T(8,128)(2,1)S(1)} async-done(((bf16[32,128,160]{1,2,0:T(8,128)(2,1)}), bf16[32,128,160]{1,2,0:T(8,128)(2,1)S(1)}, u32[]{:S(2)}, u32[]{:S(2)}) %all-to-all-start) | async-done | bytes 1310752 | tf_op jit(solution)/shard_map/all_to_all | solution.py:219
  505.9 1.4 copy.115
  (116 shorter events, 29.1 us)
Async XLA Ops:
  7.2 13.7 %copy-start = (s32[32]{0:T(128)S(1)}, s32[32]{0:T(128)}, u32[]{:S(2)}) copy-start(s32[32]{0:T(128)} %param.20) | copy-start | bytes 388
  7.2 14.9 %copy-start.15 = (f32[128]{0:T(128)S(1)}, f32[128]{0:T(128)}, u32[]{:S(2)}) copy-start(f32[128]{0:T(128)} %param.16) | copy-start | bytes 1540
  7.2 14.9 %copy-start.16 = (f32[128]{0:T(128)S(1)}, f32[128]{0:T(128)}, u32[]{:S(2)}) copy-start(f32[128]{0:T(128)} %param.17) | copy-start | bytes 1540
  7.2 14.9 %copy-start.3 = (bf16[128,2560]{1,0:T(8,128)(2,1)S(1)}, bf16[128,2560]{1,0:T(8,128)(2,1)}, u32[]{:S(2)}) copy-start(bf16[128,2560]{1,0:T(8,128)(2,1)} %param.15) | copy-start | bytes 1966084
  7.2 81.0 %all-gather.6.cloned.1.call-start = ((), (), s32[]{:S(2)}) async-start(), calls=%async_computation.8 | async-start | bytes 4456448 | tf_op jit(solution)/shard_map/all_gather | solution.py:38
  14.4 183.9 %reduce-scatter.3.cloned.1.call-start = ((), (), s32[]{:S(2)}) async-start(), calls=%async_computation.6 | async-start | bytes 4456448 | tf_op jit(solution)/shard_map/reduce_scatter | solution.py:55
  93.6 1.3 copy-start.9
  95.6 0.9 copy-start.10
  97.2 0.9 copy-start.11
  98.8 0.9 copy-start.12
  108.0 1.2 copy-start.5
  110.0 0.9 copy-start.6
  111.7 0.9 copy-start.7
  113.3 0.9 copy-start.8
  123.2 108.4 %copy-start.2 = (bf16[128,5120]{1,0:T(8,128)(2,1)S(1)}, bf16[128,5120]{1,0:T(8,128)(2,1)}, u32[]{:S(2)}) copy-start(bf16[128,5120]{1,0:T(8,128)(2,1)} %param.12) | copy-start | bytes 3932164
  123.2 108.4 %reduce-scatter.5.cloned.1.call-start = ((), (), s32[]{:S(2)}) async-start(), calls=%async_computation.7 | async-start | bytes 393216 | tf_op jit(solution)/shard_map/reduce_scatter | solution.py:55
  198.3 189.1 %all-gather.8.cloned.1.call-start = ((), (), s32[]{:S(2)}) async-start(), calls=%async_computation.9 | async-start | bytes 4325376 | tf_op jit(solution)/shard_map/all_gather | solution.py:215
  321.9 98.8 %copy-start.4 = (bf16[160,512]{1,0:T(8,128)(2,1)S(1)}, bf16[160,512]{1,0:T(8,128)(2,1)}, u32[]{:S(2)}) copy-start(bf16[160,512]{1,0:T(8,128)(2,1)} %param.21) | copy-start | bytes 491524
  321.9 98.8 %copy-start.13 = (bf16[10,512]{1,0:T(8,128)(2,1)S(1)}, bf16[10,512]{1,0:T(8,128)(2,1)}, u32[]{:S(2)}) copy-start(bf16[10,512]{1,0:T(8,128)(2,1)} %param.23) | copy-start | bytes 30724
  321.9 98.8 %copy-start.14 = (bf16[10,512]{1,0:T(8,128)(2,1)S(1)}, bf16[10,512]{1,0:T(8,128)(2,1)}, u32[]{:S(2)}) copy-start(bf16[10,512]{1,0:T(8,128)(2,1)} %param.22) | copy-start | bytes 30724
  391.2 29.5 %all-to-all-start.2 = ((bf16[16,10,512]{2,1,0:T(8,128)(2,1)}), bf16[16,10,512]{2,1,0:T(8,128)(2,1)S(1)}, u32[]{:S(2)}, u32[]{:S(2)}) async-start(bf16[16,10,512]{2,1,0:T(8,128)(2,1)} %reshape.265), calls=%async_computation.4 | async-start | bytes 524288 | tf_op jit(solution)/shard_map/all_to_all | solution.py:71
  422.1 13.0 %all-to-all-start.3 = ((bf16[16,10,512]{2,1,0:T(8,128)(2,1)}), bf16[16,10,512]{2,1,0:T(8,128)(2,1)S(1)}, u32[]{:S(2)}, u32[]{:S(2)}) async-start(bf16[16,10,512]{2,1,0:T(8,128)(2,1)} %broadcast_in_dim.19), calls=%async_computation.5 | async-start | bytes 524288 | tf_op jit(solution)/shard_map/all_to_all | solution.py:77
  435.1 72.2 %copy-start.1 = (s32[32]{0:T(128)S(1)}, s32[32]{0:T(128)}, u32[]{:S(2)}) copy-start(s32[32]{0:T(128)} %param.20) | copy-start | bytes 388
  435.1 70.8 %all-to-all-start = ((bf16[32,128,160]{1,2,0:T(8,128)(2,1)}), bf16[32,128,160]{1,2,0:T(8,128)(2,1)S(1)}, u32[]{:S(2)}, u32[]{:S(2)}) async-start(bf16[32,128,160]{1,2,0:T(8,128)(2,1)} %bitcast.100), calls=%async_computation.2 | async-start | bytes 2621440 | tf_op jit(solution)/shard_map/all_to_all | solution.py:219
Sparse Core Ops, SparseCore 0:
  14.5 73.6 all-gather.5
  123.3 74.8 reduce-scatter.2
  201.0 30.5 reduce-scatter.4
  233.7 153.5 all-gather.7
where the time goes:
time: 515 us; the launch traced here: 514 us
  waiting for transfers between devices  309 us (60%)
  blocking collectives  96.6 us (19%)
  local copies, waits for them, and re-layouts  31.3 us (6%)
  starting transfers between devices  30.8 us (6%)
  matrix products  18.5 us (4%)
  between operations  14.3 us (3%)
  other arithmetic  13.2 us (3%)
    reduce_scatter x2, waiting for transfers between devices, reduced_to_own(): pieces = lax.psum_scatter(pieces, axes[k], scatter_dimension=0, tiled=True)  108 us
    all_to_all x1, blocking collectives, shards(): lax.all_to_all(attn_inputs, FSDP, split_axis=1, concat_axis=0, tiled=True)  89.5 us
    all_gather x1, waiting for transfers between devices, shards(): values_grad = lax.all_gather(own_grad, FSDP, axis=0, tiled=True)  65.4 us
    all_to_all x1, waiting for transfers between devices, shards(): lax.all_to_all(grad_cols, FSDP, split_axis=0, concat_axis=1, tiled=True)  64.5 us
    all_gather x1, waiting for transfers between devices, all_blocks(): pieces = lax.all_gather(pieces, axes[k])  58.6 us
    all_to_all x1, starting transfers between devices, sum_at_owner(): lax.all_to_all(pieces, axis, split_axis=0, concat_axis=0, tiled=True)  20.8 us
  transfers between devices with their start and end apart: 7, of which 7 were waited for; matrix products, arithmetic and copies ran while one was open for 4% of the time, Pallas kernels for 0%

commit v1 on v0

v1 whole, which is shorter than its diff:
```python
import functools
import math

import jax
import jax.numpy as jnp
from jax import lax
from jax.experimental import pallas as pl
from jax.experimental.pallas import tpu as pltpu
from jax.sharding import Mesh
from jax.sharding import PartitionSpec as P

AXES = ("xl", "z", "y", "xh", "core")
FSDP = ("xl", "z")
SIDE = ("y", "xh", "core")
SIDE_FSDP = SIDE + FSDP
FSDP_SIDE = FSDP + SIDE
MESH = pl.DeviceIdType.MESH
NZ = 16
KVH = 4
PER = 5
HEAD = 128
QB = PER * 128
EXP_SCALE = math.log2(math.e) / math.sqrt(HEAD)
LOW = -1e30

clip_low = 0.8
clip_high = 1.2
decay_first = 0.9
decay_second = 0.95
step_rate = 0.001
weight_decay = 0.1
adam_eps = 1e-08
bias_first = 1.0 - 0.9**10
bias_second = 1.0 - 0.95**10


def coefficient_row(new_ref, old_ref, rew_ref, gid_ref, len_ref, side, first_pos):
    rew = rew_ref[...]
    gid = gid_ref[...]
    lens = len_ref[...]
    roll_of = lax.broadcasted_iota(jnp.int32, rew.shape, 1)
    adv_parts, len_parts = [], []
    for roll in range(2):
        own = roll_of == side * 2 + roll
        own_gid = jnp.sum(jnp.where(own, gid, 0), axis=1, keepdims=True)
        own_rew = jnp.sum(jnp.where(own, rew, 0.0), axis=1, keepdims=True)
        own_len = jnp.sum(jnp.where(own, lens, 0), axis=1, keepdims=True)
        member = jnp.where(gid == own_gid, 1.0, 0.0)
        count = jnp.maximum(jnp.sum(member, axis=1, keepdims=True), 1.0)
        mean = jnp.sum(member * rew, axis=1, keepdims=True) / count
        spread = rew - mean
        var = jnp.sum(member * (spread * spread), axis=1, keepdims=True) / count
        adv_parts.append((own_rew - mean) / jnp.maximum(jnp.sqrt(var), 1.0))
        len_parts.append(own_len)
    slot = lax.broadcasted_iota(jnp.int32, (1, 128), 1)
    first = slot < 64
    adv = jnp.where(first, adv_parts[0], adv_parts[1])
    length = jnp.where(first, len_parts[0], len_parts[1])
    pos = first_pos + jnp.where(first, slot, slot - 64)
    ratio = jnp.exp(new_ref[...] - old_ref[...])
    clipped = jnp.minimum(jnp.maximum(ratio, clip_low), clip_high)
    active = (ratio * adv <= clipped * adv) & (pos < length)
    return jnp.where(active, -adv * ratio * (2048.0 / length.astype(jnp.float32)), 0.0)


def attention_kernel(
    q_ref,
    g_ref,
    k_ref,
    new_ref,
    old_ref,
    rew_ref,
    gid_ref,
    len_ref,
    vg_ref,
    kbuf,
    gsend,
    qst,
    gst,
    qh,
    gh,
    eb,
    mst,
    mrow,
    lrow,
    pbuf,
    rsend,
    rrecv,
    vsend,
    x_send,
    x_recv,
    ag_send,
    ag_recv,
    rs_send,
    rs_recv,
):
    xl = lax.axis_index("xl")
    z = lax.axis_index("z")
    side = (lax.axis_index("y") * 2 + lax.axis_index("xh")) * 2 + lax.axis_index("core")
    up = lax.rem(z + 1, NZ)
    down = lax.rem(z + NZ - 1, NZ)
    mine = pl.ds(pl.multiple_of(64 * xl, 64), 64)
    theirs = pl.ds(pl.multiple_of(64 * (1 - xl), 64), 64)

    barrier = pltpu.get_barrier_semaphore()
    pl.semaphore_signal(barrier, inc=1, device_id={"xl": 1 - xl}, device_id_type=MESH)
    pl.semaphore_signal(barrier, inc=1, device_id={"z": up}, device_id_type=MESH)
    pl.semaphore_signal(barrier, inc=1, device_id={"z": down}, device_id_type=MESH)
    kbuf[z, xl] = k_ref[mine, :]
    pl.semaphore_wait(barrier, 3)

    def pair_copy(src, dst, at):
        return pltpu.make_async_remote_copy(
            src_ref=src,
            dst_ref=dst,
            send_sem=x_send.at[at],
            recv_sem=x_recv.at[at],
            device_id={"xl": 1 - xl},
            device_id_type=MESH,
        )

    def ring(way):
        return {"z": up if way == 0 else down}

    def key_copy(way, step, half):
        back = step - 1
        block = lax.rem(z + NZ - back, NZ) if way == 0 else lax.rem(z + back, NZ)
        return pltpu.make_async_remote_copy(
            src_ref=kbuf.at[block, half],
            dst_ref=kbuf.at[block, half],
            send_sem=ag_send.at[way, back, half],
            recv_sem=ag_recv.at[way, back, half],
            device_id=ring(way),
            device_id_type=MESH,
        )

    def part_copy(way, step, half):
        return pltpu.make_async_remote_copy(
            src_ref=rsend.at[way, step, half],
            dst_ref=rrecv.at[way, step, half],
            send_sem=rs_send.at[way, step, half],
            recv_sem=rs_recv.at[way, step, half],
            device_id=ring(way),
            device_id_type=MESH,
        )

    key_pair = pair_copy(k_ref.at[theirs], kbuf.at[z, xl], 0)
    query_pair = pair_copy(q_ref.at[theirs], qst, 1)
    grad_pair = pair_copy(gsend.at[theirs], gst, 2)
    key_pair.start()
    for way in range(2):
        key_copy(way, 1, xl).start()
    query_pair.start()

    coeff = coefficient_row(
        new_ref, old_ref, rew_ref, gid_ref, len_ref, side, (xl * NZ + z) * 64
    )
    diag = lax.broadcasted_iota(jnp.int32, (128, 128), 0) == lax.broadcasted_iota(
        jnp.int32, (128, 128), 1
    )
    coeff_col = jnp.sum(jnp.where(diag, coeff, 0.0), axis=1, keepdims=True)
    for head in range(KVH * PER):
        cols = slice(head * HEAD, (head + 1) * HEAD)
        gsend[:, cols] = (coeff_col * g_ref[:, cols].astype(jnp.float32)).astype(jnp.bfloat16)
    grad_pair.start()

    key_pair.wait_recv()
    for way in range(2):
        key_copy(way, 1, 1 - xl).start()

    def spread(dst, src, rows, half):
        for head in range(KVH * PER):
            at = pl.ds(pl.multiple_of(64 * half, 64) + (head % PER) * 128, 64)
            dst[head // PER, at, :] = src[rows, head * HEAD : (head + 1) * HEAD]

    spread(qh, q_ref, mine, xl)
    spread(gh, gsend, mine, xl)
    mrow[...] = jnp.full(mrow.shape, LOW, jnp.float32)
    lrow[...] = jnp.zeros(lrow.shape, jnp.float32)

    def arrived(step):
        for way in range(2):
            if way == 1 and step == 8:
                continue
            for half in range(2):
                key_copy(way, step, half).wait_recv()
                if step < (8 if way == 0 else 7):
                    key_copy(way, step + 1, half).start()

    row = lax.broadcasted_iota(jnp.int32, (256, 1), 0)
    lane = lax.broadcasted_iota(jnp.int32, (1, QB), 1)
    in_head = lax.rem(lane, 128)
    qpos = jnp.where(in_head < 64, in_head, in_head - 64 + 1024) + z * 64
    in_block = lax.rem(row, 128)
    kpos_base = jnp.where(in_block < 64, in_block, in_block - 64 + 1024)

    def score(index, carry):
        t = index // KVH + 1
        head = lax.rem(index, KVH)
        cols = pl.ds(pl.multiple_of(head * HEAD, HEAD), HEAD)
        a = lax.rem(z + NZ - t, NZ)
        b = lax.rem(z + jnp.where(t == 8, 0, t), NZ)
        keys = jnp.concatenate(
            [
                kbuf[a, :, :, cols].reshape(128, HEAD),
                kbuf[b, :, :, cols].reshape(128, HEAD),
            ],
            axis=0,
        )
        s = lax.dot_general(
            keys, qh[head], (((1,), (1,)), ((), ())), preferred_element_type=jnp.float32
        )
        kpos = kpos_base + jnp.where(row < 128, a, b) * 64
        s = jnp.where(kpos <= qpos, s, LOW)
        old = mrow[head]
        top = jnp.maximum(old, jnp.max(s, axis=0, keepdims=True))
        e = jnp.exp2((s - top) * EXP_SCALE)
        lrow[head] = lrow[head] * jnp.exp2((old - top) * EXP_SCALE) + jnp.sum(
            e, axis=0, keepdims=True
        )
        mrow[head] = top
        mst[t - 1, head] = top
        eb[t - 1, head] = e.astype(jnp.bfloat16)
        return carry

    def scores(first, last):
        lax.fori_loop((first - 1) * KVH, last * KVH, score, 0)

    for step in range(1, 4):
        arrived(step)
    query_pair.wait_recv()
    spread(qh, qst, slice(None), 1 - xl)
    arrived(4)
    scores(1, 2)
    arrived(5)
    scores(3, 4)
    arrived(6)
    scores(5, 5)
    arrived(7)
    scores(6, 7)
    grad_pair.wait_recv()
    spread(gh, gst, slice(None), 1 - xl)
    arrived(8)
    scores(8, 8)

    def part(t, which, slot):
        def one(head, carry):
            cols = pl.ds(pl.multiple_of(head * HEAD, HEAD), HEAD)
            scale = jnp.exp2((mst[t - 1, head] - mrow[head]) * EXP_SCALE) / lrow[head]
            p = eb[t - 1, head, pl.ds(which * 128, 128), :].astype(jnp.float32) * scale
            pbuf[slot, :, cols] = jnp.dot(
                p.astype(jnp.bfloat16), gh[head], preferred_element_type=jnp.float32
            )
            return carry

        lax.fori_loop(0, KVH, one, 0)

    def pass_on(way, step):
        for half in range(2):
            value = pbuf[way, half * 64 : (half + 1) * 64, :]
            if step > 0:
                part_copy(way, step - 1, half).wait_recv()
                value = value + rrecv[way, step - 1, half].astype(jnp.float32)
            rsend[way, step, half] = value.astype(jnp.bfloat16)
            part_copy(way, step, half).start()

    for step in range(8):
        part(8 - step, 0 if step == 0 else 1, 0)
        pass_on(0, step)
        if step < 7:
            part(7 - step, 0, 1)
            pass_on(1, step)
    part(8, 1, 0)
    value_pair = pair_copy(vsend, vg_ref.at[pl.ds(pl.multiple_of(64 * xl, 64), 64)], 3)
    for half in range(2):
        part_copy(1, 6, half).wait_recv()
        part_copy(0, 7, half).wait_recv()
    own = pl.ds(pl.multiple_of(64 * xl, 64), 64)
    other = pl.ds(pl.multiple_of(64 * (1 - xl), 64), 64)
    vsend[...] = (
        pbuf[0, other, :]
        + rrecv[1, 6, 1 - xl].astype(jnp.float32)
        + rrecv[0, 7, 1 - xl].astype(jnp.float32)
    ).astype(jnp.bfloat16)
    value_pair.start()
    vg_ref[own, :] = (
        pbuf[0, own, :]
        + rrecv[1, 6, xl].astype(jnp.float32)
        + rrecv[0, 7, xl].astype(jnp.float32)
    ).astype(jnp.bfloat16)
    for way in range(2):
        for step in range(8 - way):
            for half in range(2):
                key_copy(way, step + 1, half).wait_send()
                part_copy(way, step, half).wait_send()
    key_pair.wait_send()
    query_pair.wait_send()
    grad_pair.wait_send()
    value_pair.wait()


def value_gradients(queries, logp_grad, key_vectors, new_logp, old_logp, rewards, gids, lengths):
    vmem = pl.BlockSpec(memory_space=pltpu.VMEM)
    dma = pltpu.SemaphoreType.DMA
    bf, f32 = jnp.bfloat16, jnp.float32
    return pl.pallas_call(
        attention_kernel,
        out_shape=jax.ShapeDtypeStruct((128, 512), bf),
        in_specs=[vmem] * 8,
        out_specs=vmem,
        scratch_shapes=[
            pltpu.VMEM((NZ, 2, 64, 512), bf),
            pltpu.VMEM((128, 2560), bf),
            pltpu.VMEM((64, 2560), bf),
            pltpu.VMEM((64, 2560), bf),
            pltpu.VMEM((KVH, QB, HEAD), bf),
            pltpu.VMEM((KVH, QB, HEAD), bf),
            pltpu.VMEM((8, KVH, 256, QB), bf),
            pltpu.VMEM((8, KVH, 1, QB), f32),
            pltpu.VMEM((KVH, 1, QB), f32),
            pltpu.VMEM((KVH, 1, QB), f32),
            pltpu.VMEM((2, 128, 512), f32),
            pltpu.VMEM((2, 8, 2, 64, 512), bf),
            pltpu.VMEM((2, 8, 2, 64, 512), bf),
            pltpu.VMEM((64, 512), bf),
            dma((4,)),
            dma((4,)),
            dma((2, 8, 2)),
            dma((2, 8, 2)),
            dma((2, 8, 2)),
            dma((2, 8, 2)),
        ],
        compiler_params=pltpu.CompilerParams(
            collective_id=0, has_side_effects=True, vmem_limit_bytes=48 * 1024 * 1024
        ),
    )(
        queries,
        logp_grad,
        key_vectors,
        new_logp.reshape(1, 128),
        old_logp.reshape(1, 128),
        rewards.reshape(1, 32),
        gids.reshape(1, 32),
        lengths.reshape(1, 32),
    )


def split_up(value, dim, peers):
    before, after = (value.shape[:dim], value.shape[dim + 1 :])
    return jnp.moveaxis(value.reshape(*before, peers, -1, *after), dim, 0)


def laid_out(pieces, dim):
    pieces = jnp.moveaxis(pieces, 0, dim)
    dims = pieces.shape
    return pieces.reshape(*dims[:dim], dims[dim] * dims[dim + 1], *dims[dim + 2 :])


def sum_at_owner(value, axis, dim):
    pieces = split_up(value, dim, lax.axis_size(axis))
    arrived = lax.all_to_all(pieces, axis, split_axis=0, concat_axis=0, tiled=True)
    return arrived.astype(jnp.float32).sum(axis=0)


def collect(value, axis, dim):
    peers = lax.axis_size(axis)
    pieces = lax.all_to_all(
        jnp.broadcast_to(value[None], (peers, *value.shape)), axis, 0, 0, tiled=True
    )
    return laid_out(pieces, dim)


def adam_rows(old_rows, grad_rows, first_moment, second_moment):
    first = decay_first * first_moment.astype(jnp.float32) + (1.0 - decay_first) * grad_rows
    second = (
        decay_second * second_moment.astype(jnp.float32)
        + (1.0 - decay_second) * grad_rows * grad_rows
    )
    weight_now = old_rows.astype(jnp.float32)
    update = (
        first / bias_first / (jnp.sqrt(second / bias_second) + adam_eps) + weight_decay * weight_now
    )
    return (
        (weight_now - step_rate * update).astype(jnp.bfloat16),
        first.astype(jnp.bfloat16),
        second.astype(jnp.bfloat16),
    )


def shards(
    attn_inputs,
    queries,
    key_vectors,
    logp_grad,
    new_logp,
    old_logp,
    rewards,
    group_ids,
    lengths,
    value_proj,
    first_moment,
    second_moment,
):
    side_index = lax.axis_index(SIDE)
    own_grad = value_gradients(
        queries, logp_grad, key_vectors, new_logp, old_logp, rewards, group_ids, lengths
    )
    in_columns = lax.all_to_all(attn_inputs, FSDP, split_axis=1, concat_axis=0, tiled=True)
    values_grad = lax.all_gather(own_grad, FSDP, axis=0, tiled=True)
    weights = lax.all_gather(value_proj, FSDP, axis=0, tiled=True)
    input_grad = jnp.dot(own_grad, weights.T, preferred_element_type=jnp.float32).astype(
        jnp.bfloat16
    )
    weight_grad = lax.dot_general(
        in_columns, values_grad, (((0,), (0,)), ((), ())), preferred_element_type=jnp.float32
    )
    shard_grad = sum_at_owner(weight_grad.astype(jnp.bfloat16), SIDE, 0)
    shard_rows = shard_grad.shape[0]
    old_rows = lax.dynamic_slice_in_dim(value_proj, side_index * shard_rows, shard_rows, 0)
    new_rows, new_first, new_second = adam_rows(old_rows, shard_grad, first_moment, second_moment)
    new_proj = collect(new_rows, SIDE, 0)
    return (input_grad, new_proj, new_first, new_second)


def solution(mesh):
    torus = Mesh(mesh.devices.reshape(2, 16, 4, 2, 2), AXES)
    placed = (
        P(SIDE_FSDP, None),
        P(SIDE_FSDP, None),
        P(SIDE_FSDP, None),
        P(SIDE_FSDP, None),
        P(SIDE_FSDP),
        P(SIDE_FSDP),
        P(),
        P(),
        P(),
        P(FSDP, None),
        P(FSDP_SIDE, None),
        P(FSDP_SIDE, None),
    )
    return jax.shard_map(
        shards,
        mesh=torus,
        in_specs=placed,
        out_specs=(P(SIDE_FSDP, None), P(FSDP, None), P(FSDP_SIDE, None), P(FSDP_SIDE, None)),
        check_vma=False,
    )
```

time: 515 us -> 409 us (0.79)
  the two profiles are of different devices: /device:TPU:33 before, /device:TPU:8 now
where the time goes in v1:
time: 409 us; the launch traced here: 408 us
  waiting for transfers between devices  187 us (46%)
  blocking collectives  93.2 us (23%)
  Pallas kernels  87.5 us (21%)
  between operations  14.1 us (3%)
  local copies, waits for them, and re-layouts  8.64 us (2%)
  starting transfers between devices  8.46 us (2%)
  matrix products  8.45 us (2%)
    all_gather x1, waiting for transfers between devices, shards(): weights = lax.all_gather(value_proj, FSDP, axis=0, tiled=True)  101 us
    pallas_call x1, Pallas kernels, value_gradients(): pl.pallas_call(attention_kernel, out_shape=jax.ShapeDtypeStruct((128, 512...  87.5 us
    all_to_all x1, blocking collectives, shards(): lax.all_to_all(attn_inputs, FSDP, split_axis=1, concat_axis=0, tiled=True)  79 us
    all_gather x1, waiting for transfers between devices, shards(): values_grad = lax.all_gather(own_grad, FSDP, axis=0, tiled=True)  75.7 us
    all_to_all x1, blocking collectives, collect(): lax.all_to_all(jnp.broadcast_to(value[None], (peers, *value.shape)), axis...  14.2 us
    all_to_all x1, waiting for transfers between devices, sum_at_owner(): lax.all_to_all(pieces, axis, split_axis=0, concat_axis=0, tiled=True)  8.73 us
    all_to_all x1, starting transfers between devices, sum_at_owner(): lax.all_to_all(pieces, axis, split_axis=0, concat_axis=0, tiled=True)  8.38 us
  transfers between devices with their start and end apart: 3, of which 3 were waited for; matrix products, arithmetic and copies ran while one was open for 2% of the time, Pallas kernels for 0%

profile of v1, /device:TPU:8, one launch (start us, length us, event | category | flops | bytes accessed | tf_op | source)
XLA Modules:
  0.0 408.4 jit_solution(1442301887561918360)
XLA Ops:
  7.2 0.0 all-gather.5.cloned.1.call-start
  7.2 0.0 copy-start
  7.2 1.1 copy-done
  8.3 0.0 copy-start.1
  8.3 1.1 copy-done.1
  9.4 0.0 copy-start.2
  9.4 0.9 copy-done.2
  10.3 0.7 copy-done.3
  11.0 0.7 copy-done.4
  11.6 0.7 copy-done.5
  12.3 0.7 copy-done.6
  12.9 0.7 copy-done.7
  13.6 87.5 %shard_map.147 = bf16[128,512]{1,0:T(8,128)(2,1)} custom-call(bf16[128,2560]{1,0:T(8,128)(2,1)S(1)} %copy-done, bf16[128,2560]{1,0:T(8,128)(2,1)S(1)} %copy-done.1, bf16[128,512]{1,0:T(8,128)(2,1)S(1)} %copy-done.2, f32[1,128]{1,0:T(1,128)S(1)} %bitcast.23, f32[1,128]{1,0:T(1,128)S(1)} %bitcast.24, f32[1,32]{1,0:T(1,128)S(1)} %bitcast.25, ...), custom_call_target="tpu_custom_call" | custom-call | tf_op jit(solution)/shard_map/pallas_call | solution.py:306
  101.1 0.0 all-gather.5.cloned.1.call-update
  101.1 0.0 all-gather.3.cloned.1.call-start
  101.2 0.7 all-gather.3.cloned.1.call-update
  101.9 0.0 copy-done.8
  101.9 0.8 copy.16
  102.7 79.0 %all_to_all.29 = bf16[128,32,160]{0,2,1:T(8,128)(2,1)S(1)} all-to-all(bf16[128,32,160]{0,2,1:T(8,128)(2,1)S(1)} %bitcast.28), channel_id=1, replica_groups=mesh['xl'=2,'z'=16,'y'=4,'xh'=2,'core'=2] {'xl','z'}, dimensions={1} | all-to-all | bytes 2621440 | tf_op jit(solution)/shard_map/all_to_all | solution.py:408
  181.7 75.7 %all-gather.5.cloned.1.call-done = bf16[4096,512]{1,0:T(8,128)(2,1)} async-done(((bf16[128,512]{1,0:T(8,128)(2,1)}), bf16[4096,512]{1,0:T(8,128)(2,1)}) %all-gather.5.cloned.1.call-update) | async-done | bytes 4194320 | tf_op jit(solution)/shard_map/all_gather | solution.py:409
  257.3 3.0 fusion.6
  260.4 0.8 reshape.38
  261.1 8.4 %all-to-all-start.1 = ((bf16[16,10,512]{2,1,0:T(8,128)(2,1)}), bf16[16,10,512]{2,1,0:T(8,128)(2,1)S(1)}, u32[]{:S(2)}, u32[]{:S(2)}) async-start(bf16[16,10,512]{2,1,0:T(8,128)(2,1)} %reshape.38), calls=%async_computation.1 | async-start | bytes 524288 | tf_op jit(solution)/shard_map/all_to_all | solution.py:361
  269.5 8.7 %all-to-all-done.1 = bf16[16,10,512]{2,1,0:T(8,128)(2,1)S(1)} async-done(((bf16[16,10,512]{2,1,0:T(8,128)(2,1)}), bf16[16,10,512]{2,1,0:T(8,128)(2,1)S(1)}, u32[]{:S(2)}, u32[]{:S(2)}) %all-to-all-start.1) | async-done | bytes 163872 | tf_op jit(solution)/shard_map/all_to_all | solution.py:361
  278.3 0.1 convert_reduce_fusion
  278.3 0.0 copy-done.9
  278.3 0.0 copy-done.10
  278.3 1.4 fusion.14
  279.7 14.2 %all_to_all.30 = bf16[16,10,512]{2,1,0:T(8,128)(2,1)S(1)} all-to-all(bf16[16,10,512]{2,1,0:T(8,128)(2,1)S(1)} %broadcast_in_dim.2), channel_id=1, replica_groups=mesh['xl'=2,'z'=16,'y'=4,'xh'=2,'core'=2] {'y','xh','core'}, dimensions={0} | all-to-all | bytes 327680 | tf_op jit(solution)/shard_map/all_to_all | solution.py:367
  294.0 0.7 reshape.39
  294.7 101.4 %all-gather.3.cloned.1.call-done = bf16[5120,512]{1,0:T(8,128)(2,1)} async-done(((bf16[160,512]{1,0:T(8,128)(2,1)}), bf16[5120,512]{1,0:T(8,128)(2,1)}) %all-gather.3.cloned.1.call-update) | async-done | bytes 5242896 | tf_op jit(solution)/shard_map/all_gather | solution.py:410
  396.1 5.4 %convolution_convert_fusion = bf16[128,5120]{1,0:T(8,128)(2,1)} fusion(bf16[128,512]{1,0:T(8,128)(2,1)} %shard_map.147, bf16[5120,512]{1,0:T(8,128)(2,1)} %all-gather.3.cloned.1.call-done), kind=kOutput, calls=%fused_computation | convolution fusion | flops 671744000 | bytes 6684672 | tf_op jit(solution)/shard_map/dot_general | solution.py:411
  (9 shorter events, 0.0 us)
Async XLA Ops:
  7.2 250.2 %all-gather.5.cloned.1.call-start = ((), (), s32[]{:S(2)}) async-start(), calls=%async_computation.4 | async-start | bytes 4325376 | tf_op jit(solution)/shard_map/all_gather | solution.py:409
  7.2 1.1 copy-start
  8.3 1.1 copy-start.1
  9.4 0.9 copy-start.2
  10.3 0.7 copy-start.3
  11.0 0.7 copy-start.4
  11.6 0.7 copy-start.5
  12.3 0.7 copy-start.6
  12.9 0.7 copy-start.7
  13.6 88.3 %copy-start.8 = (bf16[128,5120]{1,0:T(8,128)(2,1)S(1)}, bf16[128,5120]{1,0:T(8,128)(2,1)}, u32[]{:S(2)}) copy-start(bf16[128,5120]{1,0:T(8,128)(2,1)} %param.12) | copy-start | bytes 3932164
  101.1 295.0 %all-gather.3.cloned.1.call-start = ((), (), s32[]{:S(2)}) async-start(), calls=%async_computation.3 | async-start | bytes 5406720 | tf_op jit(solution)/shard_map/all_gather | solution.py:410
  181.7 96.6 %copy-start.9 = (bf16[10,512]{1,0:T(8,128)(2,1)S(1)}, bf16[10,512]{1,0:T(8,128)(2,1)}, u32[]{:S(2)}) copy-start(bf16[10,512]{1,0:T(8,128)(2,1)} %param.23) | copy-start | bytes 30724
  181.7 96.6 %copy-start.10 = (bf16[10,512]{1,0:T(8,128)(2,1)S(1)}, bf16[10,512]{1,0:T(8,128)(2,1)}, u32[]{:S(2)}) copy-start(bf16[10,512]{1,0:T(8,128)(2,1)} %param.22) | copy-start | bytes 30724
  261.1 17.1 %all-to-all-start.1 = ((bf16[16,10,512]{2,1,0:T(8,128)(2,1)}), bf16[16,10,512]{2,1,0:T(8,128)(2,1)S(1)}, u32[]{:S(2)}, u32[]{:S(2)}) async-start(bf16[16,10,512]{2,1,0:T(8,128)(2,1)} %reshape.38), calls=%async_computation.1 | async-start | bytes 524288 | tf_op jit(solution)/shard_map/all_to_all | solution.py:361
Sparse Core Ops, SparseCore 0:
  101.2 156.0 all-gather.4
  259.4 136.6 all-gather.2

commit v2 on v1

v2 whole, which is shorter than its diff:
```python
import math

import jax
import jax.numpy as jnp
from jax import lax
from jax.experimental import pallas as pl
from jax.experimental.pallas import tpu as pltpu
from jax.sharding import Mesh
from jax.sharding import PartitionSpec as P

AXES = ("xl", "z", "y", "xh", "core")
FSDP = ("xl", "z")
SIDE = ("y", "xh", "core")
SIDE_FSDP = SIDE + FSDP
FSDP_SIDE = FSDP + SIDE
MESH = pl.DeviceIdType.MESH
NZ = 16
KVH = 4
PER = 5
HEAD = 128
QB = PER * 128
EXP_SCALE = math.log2(math.e) / math.sqrt(HEAD)
LOW = -1e30

clip_low = 0.8
clip_high = 1.2
decay_first = 0.9
decay_second = 0.95
step_rate = 0.001
weight_decay = 0.1
adam_eps = 1e-08
bias_first = 1.0 - 0.9**10
bias_second = 1.0 - 0.95**10


def coefficient_row(new_ref, old_ref, rew_ref, gid_ref, len_ref, side, first_pos):
    rew = rew_ref[...]
    gid = gid_ref[...]
    lens = len_ref[...]
    roll_of = lax.broadcasted_iota(jnp.int32, rew.shape, 1)
    adv_parts, len_parts = [], []
    for roll in range(2):
        own = roll_of == side * 2 + roll
        own_gid = jnp.sum(jnp.where(own, gid, 0), axis=1, keepdims=True)
        own_rew = jnp.sum(jnp.where(own, rew, 0.0), axis=1, keepdims=True)
        own_len = jnp.sum(jnp.where(own, lens, 0), axis=1, keepdims=True)
        member = jnp.where(gid == own_gid, 1.0, 0.0)
        count = jnp.maximum(jnp.sum(member, axis=1, keepdims=True), 1.0)
        mean = jnp.sum(member * rew, axis=1, keepdims=True) / count
        spread = rew - mean
        var = jnp.sum(member * (spread * spread), axis=1, keepdims=True) / count
        adv_parts.append((own_rew - mean) / jnp.maximum(jnp.sqrt(var), 1.0))
        len_parts.append(own_len)
    slot = lax.broadcasted_iota(jnp.int32, (1, 128), 1)
    first = slot < 64
    adv = jnp.where(first, adv_parts[0], adv_parts[1])
    length = jnp.where(first, len_parts[0], len_parts[1])
    pos = first_pos + jnp.where(first, slot, slot - 64)
    ratio = jnp.exp(new_ref[...] - old_ref[...])
    clipped = jnp.minimum(jnp.maximum(ratio, clip_low), clip_high)
    active = (ratio * adv <= clipped * adv) & (pos < length)
    return jnp.where(active, -adv * ratio * (2048.0 / length.astype(jnp.float32)), 0.0)


def adam_rows(weight_now, grad_rows, first_moment, second_moment):
    first = decay_first * first_moment + (1.0 - decay_first) * grad_rows
    second = decay_second * second_moment + (1.0 - decay_second) * grad_rows * grad_rows
    update = (
        first / bias_first / (jnp.sqrt(second / bias_second) + adam_eps) + weight_decay * weight_now
    )
    return weight_now - step_rate * update, first, second


def kernel(
    x_hbm,
    q_hbm,
    k_hbm,
    g_hbm,
    new_hbm,
    old_hbm,
    rew_hbm,
    gid_hbm,
    len_hbm,
    w_hbm,
    m1_ref,
    m2_ref,
    ig_ref,
    np_ref,
    nf_ref,
    ns_ref,
    qv,
    gv,
    kv,
    xv,
    wv,
    newv,
    oldv,
    rewv,
    gidv,
    lenv,
    kbuf,
    gsend,
    qst,
    gst,
    qh,
    gh,
    eb,
    mst,
    mrow,
    lrow,
    pbuf,
    rsend,
    rrecv,
    vsend,
    vrecv,
    xt,
    xg,
    wfull,
    mv,
    moms,
    m1f,
    m2f,
    vga,
    acc,
    xs,
    xr,
    zsum,
    zs,
    zr,
    gy,
    gf,
    load_sem,
    x_send,
    x_recv,
    ag_send,
    ag_recv,
    rs_send,
    rs_recv,
    in_send,
    in_recv,
    wz_send,
    wz_recv,
    wy_send,
    wy_recv,
    mo_send,
    mo_recv,
    va_send,
    va_recv,
    xs_send,
    xs_recv,
    zs_send,
    zs_recv,
    gy_send,
    gy_recv,
    gf_send,
    gf_recv,
):
    xl = lax.axis_index("xl")
    z = lax.axis_index("z")
    y = lax.axis_index("y")
    xh = lax.axis_index("xh")
    core = lax.axis_index("core")
    side = (y * 2 + xh) * 2 + core
    x = xh * 2 + xl
    up = lax.rem(z + 1, NZ)
    down = lax.rem(z + NZ - 1, NZ)
    mine = pl.ds(pl.multiple_of(64 * xl, 64), 64)
    theirs = pl.ds(pl.multiple_of(64 * (1 - xl), 64), 64)

    def lanes(index):
        return pl.ds(pl.multiple_of(index * 128, 128), 128)

    def y_at(step):
        return lax.rem(y + step, 4)

    loads = [
        pltpu.make_async_copy(src, dst, load_sem.at[i])
        for i, (src, dst) in enumerate(
            (
                (k_hbm, kv),
                (q_hbm, qv),
                (w_hbm, wv),
                (new_hbm, newv),
                (old_hbm, oldv),
                (rew_hbm, rewv),
                (gid_hbm, gidv),
                (len_hbm, lenv),
                (g_hbm, gv),
                (x_hbm, xv),
            )
        )
    ]
    for load in loads:
        load.start()

    barrier = pltpu.get_barrier_semaphore()

    def greet(**where):
        pl.semaphore_signal(barrier, inc=1, device_id=where, device_id_type=MESH)

    for step in range(1, NZ):
        greet(z=lax.rem(z + step, NZ))
    for flip in range(1, 8):
        greet(xl=xl ^ (flip & 1), xh=xh ^ (flip >> 1 & 1), core=core ^ (flip >> 2))
    for step in range(1, 4):
        for flip in range(4):
            greet(y=y_at(step), xh=xh ^ (flip & 1), core=core ^ (flip >> 1))

    mv[...] = jnp.zeros(mv.shape, mv.dtype)
    mv[0:10, :] = m1_ref[...]
    mv[16:26, :] = m2_ref[...]
    moms[side] = mv[...]
    loads[0].wait()
    kbuf[z, xl] = kv[mine, :]
    for i in range(1, 3):
        loads[i].wait()
    pl.semaphore_wait(barrier, NZ - 1 + 7 + 12)

    def copy_to(src, dst, send, recv, **where):
        return pltpu.make_async_remote_copy(
            src_ref=src,
            dst_ref=dst,
            send_sem=send,
            recv_sem=recv,
            device_id=where,
            device_id_type=MESH,
        )

    def pair_copy(src, dst, at):
        return copy_to(src, dst, x_send.at[at], x_recv.at[at], xl=1 - xl)

    def ring_block(way, step):
        back = step - 1
        return lax.rem(z + NZ - back, NZ) if way == 0 else lax.rem(z + back, NZ)

    def key_copy(way, step, half):
        part = kbuf.at[ring_block(way, step), half]
        return copy_to(
            part,
            part,
            ag_send.at[way, step - 1, half],
            ag_recv.at[way, step - 1, half],
            z=up if way == 0 else down,
        )

    def weight_copy(way, step):
        part = wfull.at[core * NZ + ring_block(way, step), :, lanes(y)]
        return copy_to(
            part,
            part,
            wz_send.at[way, step - 1],
            wz_recv.at[way, step - 1],
            z=up if way == 0 else down,
        )

    def part_copy(way, step, half):
        return copy_to(
            rsend.at[way, step, half],
            rrecv.at[way, step, half],
            rs_send.at[way, step, half],
            rs_recv.at[way, step, half],
            z=up if way == 0 else down,
        )

    key_pair = pair_copy(kv.at[theirs], kbuf.at[z, xl], 0)
    query_pair = pair_copy(qv.at[theirs], qst, 1)
    grad_pair = pair_copy(gsend.at[theirs], gst, 2)
    own_weight = wfull.at[core * NZ + z, :, lanes(y)]
    weight_pair = pair_copy(wv.at[:, lanes(y)], own_weight, 3)
    key_pair.start()
    for way in range(2):
        key_copy(way, 1, xl).start()

    @pl.when(core == xl)
    def _():
        weight_pair.start()
        wfull[core * NZ + z, :, lanes(y)] = wv[:, lanes(y)]

    query_pair.start()

    for i in range(3, 9):
        loads[i].wait()
    coeff = coefficient_row(newv, oldv, rewv, gidv, lenv, side, (xl * NZ + z) * 64)
    diag = lax.broadcasted_iota(jnp.int32, (128, 128), 0) == lax.broadcasted_iota(
        jnp.int32, (128, 128), 1
    )
    coeff_col = jnp.sum(jnp.where(diag, coeff, 0.0), axis=1, keepdims=True)
    for head in range(KVH * PER):
        cols = slice(head * HEAD, (head + 1) * HEAD)
        gsend[:, cols] = (coeff_col * gv[:, cols].astype(jnp.float32)).astype(jnp.bfloat16)
    grad_pair.start()

    key_pair.wait_recv()
    for way in range(2):
        key_copy(way, 1, 1 - xl).start()

    @pl.when(core != xl)
    def _():
        weight_pair.wait_recv()

    for way in range(2):
        weight_copy(way, 1).start()

    def spread(dst, src, rows, half):
        for head in range(KVH * PER):
            at = pl.ds(pl.multiple_of(64 * half, 64) + (head % PER) * 128, 64)
            dst[head // PER, at, :] = src[rows, head * HEAD : (head + 1) * HEAD]

    spread(qh, qv, mine, xl)
    spread(gh, gsend, mine, xl)
    mrow[...] = jnp.full(mrow.shape, LOW, jnp.float32)
    lrow[...] = jnp.zeros(lrow.shape, jnp.float32)

    def arrived(step):
        for half in range(2):
            for way in range(2):
                if way == 1 and step == 8:
                    continue
                key_copy(way, step, half).wait_recv()
                if step < 8 - way:
                    key_copy(way, step + 1, half).start()
        for way in range(2):
            if way == 1 and step == 8:
                continue
            weight_copy(way, step).wait_recv()
            if step < 8 - way:
                weight_copy(way, step + 1).start()

    loads[9].wait()

    def turn(n, carry):
        cols = pl.ds(pl.multiple_of(n * 640, 128), 640)
        xt[n] = xv[:, cols].T.reshape(4, 160, 128)
        return carry

    def input_copies():
        copies = []
        for step in range(4):
            for flip in range(2):
                if step + flip:
                    there = core ^ flip
                    copies.append(
                        copy_to(
                            xt.at[pl.ds(4 * there, 4), y_at(step)],
                            xg.at[:, :, lanes(2 * y + core)],
                            in_send.at[step * 2 + flip],
                            in_recv.at[step * 2 + flip],
                            y=y_at(step),
                            core=there,
                        )
                    )
        return copies

    def moment_copies():
        copies = []
        for step in range(4):
            for flip in range(4):
                if step + flip:
                    copies.append(
                        copy_to(
                            mv,
                            moms.at[side],
                            mo_send.at[step * 4 + flip],
                            mo_recv.at[step * 4 + flip],
                            y=y_at(step),
                            xh=xh ^ (flip & 1),
                            core=core ^ (flip >> 1),
                        )
                    )
        return copies

    row = lax.broadcasted_iota(jnp.int32, (256, 1), 0)
    lane = lax.broadcasted_iota(jnp.int32, (1, QB), 1)
    in_head = lax.rem(lane, 128)
    qpos = jnp.where(in_head < 64, in_head, in_head - 64 + 1024) + z * 64
    in_block = lax.rem(row, 128)
    kpos_base = jnp.where(in_block < 64, in_block, in_block - 64 + 1024)

    def score(index, carry):
        t = index // KVH + 1
        head = lax.rem(index, KVH)
        a = lax.rem(z + NZ - t, NZ)
        b = lax.rem(z + jnp.where(t == 8, 0, t), NZ)
        keys = jnp.concatenate(
            [
                kbuf[a, :, :, lanes(head)].reshape(128, HEAD),
                kbuf[b, :, :, lanes(head)].reshape(128, HEAD),
            ],
            axis=0,
        )
        s = lax.dot_general(
            keys, qh[head], (((1,), (1,)), ((), ())), preferred_element_type=jnp.float32
        )
        kpos = kpos_base + jnp.where(row < 128, a, b) * 64
        s = jnp.where(kpos <= qpos, s, LOW)
        old = mrow[head]
        top = jnp.maximum(old, jnp.max(s, axis=0, keepdims=True))
        e = jnp.exp2((s - top) * EXP_SCALE)
        lrow[head] = lrow[head] * jnp.exp2((old - top) * EXP_SCALE) + jnp.sum(
            e, axis=0, keepdims=True
        )
        mrow[head] = top
        mst[t - 1, head] = top
        eb[t - 1, head] = e.astype(jnp.bfloat16)
        return carry

    def scores(first, last):
        lax.fori_loop((first - 1) * KVH, last * KVH, score, 0)

    arrived(1)
    lax.fori_loop(0, 4, turn, 0)
    arrived(2)
    lax.fori_loop(4, 8, turn, 0)
    xg[:, :, lanes(2 * y + core)] = xt[pl.ds(4 * core, 4), y]
    for copy in input_copies():
        copy.start()
    arrived(3)
    for copy in moment_copies():
        copy.start()
    query_pair.wait_recv()
    spread(qh, qst, slice(None), 1 - xl)
    arrived(4)
    scores(1, 2)
    arrived(5)
    scores(3, 4)
    arrived(6)
    scores(5, 5)
    arrived(7)
    scores(6, 7)
    grad_pair.wait_recv()
    spread(gh, gst, slice(None), 1 - xl)
    arrived(8)

    def across_y(step):
        part = wfull.at[pl.ds(NZ * core, NZ), :, lanes(y)]
        return copy_to(part, part, wy_send.at[step], wy_recv.at[step], y=y_at(step))

    def across_core():
        part = wfull.at[pl.ds(NZ * core, NZ)]
        return copy_to(part, part, wy_send.at[0], wy_recv.at[0], core=1 - core)

    for step in range(1, 4):
        across_y(step).start()
    scores(8, 8)

    def part(t, which, slot):
        def one(head, carry):
            scale = jnp.exp2((mst[t - 1, head] - mrow[head]) * EXP_SCALE) / lrow[head]
            p = eb[t - 1, head, pl.ds(which * 128, 128), :].astype(jnp.float32) * scale
            pbuf[slot, :, lanes(head)] = jnp.dot(
                p.astype(jnp.bfloat16), gh[head], preferred_element_type=jnp.float32
            )
            return carry

        lax.fori_loop(0, KVH, one, 0)

    def pass_on(way, step):
        for half in range(2):
            value = pbuf[way, half * 64 : (half + 1) * 64, :]
            if step > 0:
                part_copy(way, step - 1, half).wait_recv()
                value = value + rrecv[way, step - 1, half].astype(jnp.float32)
            rsend[way, step, half] = value.astype(jnp.bfloat16)
            part_copy(way, step, half).start()

    for step in range(8):
        part(8 - step, 0 if step == 0 else 1, 0)
        pass_on(0, step)
        if step < 7:
            part(7 - step, 0, 1)
            pass_on(1, step)
    part(8, 1, 0)

    for copy in moment_copies():
        copy.wait_recv()
    for s in range(16):
        m1f[10 * s : 10 * s + 10, :] = moms[s, 0:10, :].astype(jnp.float32)
        m2f[10 * s : 10 * s + 10, :] = moms[s, 16:26, :].astype(jnp.float32)

    value_pair = pair_copy(vsend, vrecv, 4)
    for half in range(2):
        part_copy(1, 6, half).wait_recv()
        part_copy(0, 7, half).wait_recv()
    vsend[...] = (
        pbuf[0, theirs, :]
        + rrecv[1, 6, 1 - xl].astype(jnp.float32)
        + rrecv[0, 7, 1 - xl].astype(jnp.float32)
    ).astype(jnp.bfloat16)
    value_pair.start()
    slot = 2 * y + core
    vga[slot, mine, :] = (
        pbuf[0, mine, :]
        + rrecv[1, 6, xl].astype(jnp.float32)
        + rrecv[0, 7, xl].astype(jnp.float32)
    ).astype(jnp.bfloat16)
    value_pair.wait_recv()
    vga[slot, theirs, :] = vrecv[...]

    def values_y(step):
        return copy_to(vga.at[slot], vga.at[slot], va_send.at[step], va_recv.at[step], y=y_at(step))

    def values_core(step):
        part = vga.at[2 * lax.rem(y + 4 - step, 4) + core]
        return copy_to(part, part, va_send.at[4 + step], va_recv.at[4 + step], core=1 - core)

    for step in (2, 1, 3):
        values_y(step).start()
    values_core(0).start()

    for copy in input_copies():
        copy.wait_recv()
    for step in range(1, 4):
        across_y(step).wait_recv()
    across_core().start()

    def add_inputs(step, first):
        at = lax.rem(y + 4 - step, 4)
        a = xg[:, :, pl.ds(pl.multiple_of(at * 256, 256), 256)].reshape(640, 256)
        b = vga[pl.ds(2 * at, 2)].reshape(256, 512)
        value = jnp.dot(a, b, preferred_element_type=jnp.float32)
        acc[...] = value if first else acc[...] + value

    values_core(0).wait_recv()
    add_inputs(0, True)
    for step in (1, 3, 2):
        values_y(step).wait_recv()
        values_core(step).start()
        values_core(step).wait_recv()
        add_inputs(step, False)

    def sum_x(step):
        at = lax.rem(x + step, 4)
        return copy_to(
            xs.at[step - 1],
            xr.at[step - 1],
            xs_send.at[step - 1],
            xs_recv.at[step - 1],
            xl=lax.rem(at, 2),
            xh=at // 2,
        )

    for step in (2, 1, 3):
        at = lax.rem(x + step, 4)
        xs[step - 1] = acc[:, lanes(at)].astype(jnp.bfloat16)
        sum_x(step).start()

    across_core().wait_recv()

    def grad_tile(n, carry):
        w = wfull[pl.ds(4 * n, 4)].reshape(640, 512)
        ig_ref[:, pl.ds(pl.multiple_of(n * 640, 128), 640)] = lax.dot_general(
            vga[slot], w, (((1,), (1,)), ((), ())), preferred_element_type=jnp.float32
        ).astype(jnp.bfloat16)
        return carry

    lax.fori_loop(0, 8, grad_tile, 0)

    for step in (1, 3, 2):
        sum_x(step).wait_recv()
    total = acc[:, lanes(x)]
    for step in range(3):
        total = total + xr[step].astype(jnp.float32)
    zsum[...] = total.reshape(4, 160, 128)
    zs[...] = zsum[...].astype(jnp.bfloat16)

    def sum_z(j):
        at = 4 * j + y
        far = lax.rem(z - at + NZ, NZ)
        return copy_to(zs.at[j], zr.at[far], zs_send.at[j], zs_recv.at[far], z=at)

    for j in range(4):

        @pl.when(z != 4 * j + y)
        def _(j=j):
            sum_z(j).start()

    root = lax.rem(z, 4) == y

    def spread_y(step):
        return copy_to(gy, gy, gy_send.at[step - 1], gy_recv, y=y_at(step))

    @pl.when(root)
    def _():
        total = zsum[z // 4]
        for far in range(1, NZ):
            copy_to(zs.at[0], zr.at[far], zs_send.at[0], zs_recv.at[far], z=up).wait_recv()
            total = total + zr[far].astype(jnp.float32)
        gy[...] = total.astype(jnp.bfloat16)
        for step in range(1, 4):
            spread_y(step).start()

    @pl.when(jnp.logical_not(root))
    def _():
        spread_y(1).wait_recv()

    def spread_x(to_xh, to_core):
        k = to_xh * 2 + to_core
        return copy_to(
            gy, gf.at[x], gf_send.at[k], gf_recv.at[x], xl=core, xh=to_xh, core=to_core
        )

    def is_self(to_xh, to_core):
        return (xl == core) & (xh == to_xh) & (core == to_core)

    for to_xh in range(2):
        for to_core in range(2):

            @pl.when(jnp.logical_not(is_self(to_xh, to_core)))
            def _(to_xh=to_xh, to_core=to_core):
                spread_x(to_xh, to_core).start()

    @pl.when(xl == core)
    def _():
        gf[x] = gy[...]

    for at in range(4):

        @pl.when(jnp.logical_not((xl == core) & (x == at)))
        def _(at=at):
            copy_to(gy, gf.at[at], gf_send.at[0], gf_recv.at[at], core=1 - core).wait_recv()

    for at in range(4):
        cols = slice(at * 128, (at + 1) * 128)
        new, first, second = adam_rows(
            wv[:, cols].astype(jnp.float32),
            gf[at].astype(jnp.float32),
            m1f[:, cols],
            m2f[:, cols],
        )
        np_ref[:, cols] = new.astype(jnp.bfloat16)
        m1f[:, cols] = first
        m2f[:, cols] = second
    for s in range(16):

        @pl.when(side == s)
        def _(s=s):
            nf_ref[...] = m1f[10 * s : 10 * s + 10, :].astype(jnp.bfloat16)
            ns_ref[...] = m2f[10 * s : 10 * s + 10, :].astype(jnp.bfloat16)

    for way in range(2):
        for step in range(8 - way):
            weight_copy(way, step + 1).wait_send()
            for half in range(2):
                key_copy(way, step + 1, half).wait_send()
                part_copy(way, step, half).wait_send()
    for copy in (key_pair, query_pair, grad_pair, value_pair):
        copy.wait_send()

    @pl.when(core == xl)
    def _():
        weight_pair.wait_send()

    for copy in input_copies() + moment_copies():
        copy.wait_send()
    across_core().wait_send()
    values_core(0).wait_send()
    for step in range(1, 4):
        across_y(step).wait_send()
        values_y(step).wait_send()
        values_core(step).wait_send()
        sum_x(step).wait_send()
    for j in range(4):

        @pl.when(z != 4 * j + y)
        def _(j=j):
            sum_z(j).wait_send()

    @pl.when(root)
    def _():
        for step in range(1, 4):
            spread_y(step).wait_send()

    for to_xh in range(2):
        for to_core in range(2):

            @pl.when(jnp.logical_not(is_self(to_xh, to_core)))
            def _(to_xh=to_xh, to_core=to_core):
                spread_x(to_xh, to_core).wait_send()


def shards(
    attn_inputs,
    queries,
    key_vectors,
    logp_grad,
    new_logp,
    old_logp,
    rewards,
    group_ids,
    lengths,
    value_proj,
    first_moment,
    second_moment,
):
    vmem = pl.BlockSpec(memory_space=pltpu.VMEM)
    hbm = pl.BlockSpec(memory_space=pl.ANY)
    dma = pltpu.SemaphoreType.DMA
    bf, f32, i32 = jnp.bfloat16, jnp.float32, jnp.int32

    def buf(*shape, kind=bf):
        return pltpu.VMEM(shape, kind)

    return pl.pallas_call(
        kernel,
        out_shape=(
            jax.ShapeDtypeStruct((128, 5120), bf),
            jax.ShapeDtypeStruct((160, 512), bf),
            jax.ShapeDtypeStruct((10, 512), bf),
            jax.ShapeDtypeStruct((10, 512), bf),
        ),
        in_specs=[hbm] * 10 + [vmem] * 2,
        out_specs=(vmem,) * 4,
        scratch_shapes=[
            buf(128, 2560),
            buf(128, 2560),
            buf(128, 512),
            buf(128, 5120),
            buf(160, 512),
            buf(1, 128, kind=f32),
            buf(1, 128, kind=f32),
            buf(1, 32, kind=f32),
            buf(1, 32, kind=i32),
            buf(1, 32, kind=i32),
            buf(NZ, 2, 64, 512),
            buf(128, 2560),
            buf(64, 2560),
            buf(64, 2560),
            buf(KVH, QB, HEAD),
            buf(KVH, QB, HEAD),
            buf(8, KVH, 256, QB),
            buf(8, KVH, 1, QB, kind=f32),
            buf(KVH, 1, QB, kind=f32),
            buf(KVH, 1, QB, kind=f32),
            buf(2, 128, 512, kind=f32),
            buf(2, 8, 2, 64, 512),
            buf(2, 8, 2, 64, 512),
            buf(64, 512),
            buf(64, 512),
            buf(8, 4, 160, 128),
            buf(4, 160, 1024),
            buf(32, 160, 512),
            buf(32, 512),
            buf(16, 32, 512),
            buf(160, 512, kind=f32),
            buf(160, 512, kind=f32),
            buf(8, 128, 512),
            buf(640, 512, kind=f32),
            buf(3, 640, 128),
            buf(3, 640, 128),
            buf(4, 160, 128, kind=f32),
            buf(4, 160, 128),
            buf(NZ, 160, 128),
            buf(160, 128),
            buf(4, 160, 128),
            dma((10,)),
            dma((5,)),
            dma((5,)),
            dma((2, 8, 2)),
            dma((2, 8, 2)),
            dma((2, 8, 2)),
            dma((2, 8, 2)),
            dma((8,)),
            dma((8,)),
            dma((2, 8)),
            dma((2, 8)),
            dma((4,)),
            dma((4,)),
            dma((16,)),
            dma((16,)),
            dma((8,)),
            dma((8,)),
            dma((3,)),
            dma((3,)),
            dma((4,)),
            dma((16,)),
            dma((3,)),
            dma,
            dma((4,)),
            dma((4,)),
        ],
        compiler_params=pltpu.CompilerParams(
            collective_id=0, has_side_effects=True, vmem_limit_bytes=60 * 1024 * 1024
        ),
    )(
        attn_inputs,
        queries,
        key_vectors,
        logp_grad,
        new_logp.reshape(1, 128),
        old_logp.reshape(1, 128),
        rewards.reshape(1, 32),
        group_ids.reshape(1, 32),
        lengths.reshape(1, 32),
        value_proj,
        first_moment,
        second_moment,
    )


def solution(mesh):
    torus = Mesh(mesh.devices.reshape(2, 16, 4, 2, 2), AXES)
    placed = (
        P(SIDE_FSDP, None),
        P(SIDE_FSDP, None),
        P(SIDE_FSDP, None),
        P(SIDE_FSDP, None),
        P(SIDE_FSDP),
        P(SIDE_FSDP),
        P(),
        P(),
        P(),
        P(FSDP, None),
        P(FSDP_SIDE, None),
        P(FSDP_SIDE, None),
    )
    return jax.shard_map(
        shards,
        mesh=torus,
        in_specs=placed,
        out_specs=(P(SIDE_FSDP, None), P(FSDP, None), P(FSDP_SIDE, None), P(FSDP_SIDE, None)),
        check_vma=False,
    )
```

time: 409 us -> 141 us (0.34)
  the two profiles are of different devices: /device:TPU:8 before, /device:TPU:17 now
where the time goes in v2:
time: 141 us
  Pallas kernels  136 us (96%)
  local copies, waits for them, and re-layouts  4.39 us (3%)
    pallas_call x1, Pallas kernels, shards(): pl.pallas_call(kernel, out_shape=(jax.ShapeDtypeStruct((128, 5120), bf),...  136 us
    unnamed x10, local copies, waits for them, and re-layouts  4.39 us

profile of v2, /device:TPU:17, one launch (start us, length us, event | category | flops | bytes accessed | tf_op | source)
XLA Modules:
  0.0 141.2 jit_solution(1458168491615797169)
XLA Ops:
  0.6 136.1 %shard_map.147 = (bf16[128,5120]{1,0:T(8,128)(2,1)}, bf16[160,512]{1,0:T(8,128)(2,1)}, bf16[10,512]{1,0:T(8,128)(2,1)}, bf16[10,512]{1,0:T(8,128)(2,1)}) custom-call(bf16[128,5120]{1,0:T(8,128)(2,1)} %x_hbm.1, bf16[128,2560]{1,0:T(8,128)(2,1)} %q_hbm.1, bf16[128,512]{1,0:T(8,128)(2,1)} %k_hbm.1, bf16[128,2560]{1,0:T(8,128)(2,1)} %g_hbm.1, f32[1,128]{1,0:T(1,128)} %bitcast.5, ...), custom_call_target="tpu_custom_call" | custom-call | tf_op jit(solution)/shard_map/pallas_call | solution.py:703
  136.8 0.0 copy-start
  136.8 0.0 copy-start.2
  136.8 0.0 copy-start.1
  136.8 2.5 %copy.20 = bf16[128,5120]{1,0:T(8,128)(2,1)} copy(bf16[128,5120]{1,0:T(8,128)(2,1)} %get-tuple-element.8) | data formatting | bytes 2621440
  139.3 0.0 copy-done
  139.3 0.7 copy.21
  140.0 0.0 copy-done.2
  140.0 0.6 copy.22
  140.6 0.0 copy-done.1
  140.6 0.6 copy.23
Async XLA Ops:
  136.8 2.5 %copy-start = (bf16[160,512]{1,0:T(8,128)(2,1)S(1)}, bf16[160,512]{1,0:T(8,128)(2,1)}, u32[]{:S(2)}) copy-start(bf16[160,512]{1,0:T(8,128)(2,1)} %get-tuple-element.9) | copy-start | bytes 491524
  136.8 3.2 %copy-start.2 = (bf16[10,512]{1,0:T(8,128)(2,1)S(1)}, bf16[10,512]{1,0:T(8,128)(2,1)}, u32[]{:S(2)}) copy-start(bf16[10,512]{1,0:T(8,128)(2,1)} %get-tuple-element.10) | copy-start | bytes 30724
  136.8 3.8 %copy-start.1 = (bf16[10,512]{1,0:T(8,128)(2,1)S(1)}, bf16[10,512]{1,0:T(8,128)(2,1)}, u32[]{:S(2)}) copy-start(bf16[10,512]{1,0:T(8,128)(2,1)} %get-tuple-element.11) | copy-start | bytes 30724

commit v3 on v2

--- a/solution.py
+++ b/solution.py
@@ -109,6 +109,7 @@
     mrow,
     lrow,
     pbuf,
+    pown,
     rsend,
     rrecv,
     vsend,
@@ -154,6 +155,7 @@
     gy_recv,
     gf_send,
     gf_recv,
+    known,
 ):
     xl = lax.axis_index("xl")
     z = lax.axis_index("z")
@@ -198,23 +200,31 @@
     def greet(**where):
         pl.semaphore_signal(barrier, inc=1, device_id=where, device_id_type=MESH)
 
-    for step in range(1, NZ):
-        greet(z=lax.rem(z + step, NZ))
-    for flip in range(1, 8):
-        greet(xl=xl ^ (flip & 1), xh=xh ^ (flip >> 1 & 1), core=core ^ (flip >> 2))
-    for step in range(1, 4):
-        for flip in range(4):
-            greet(y=y_at(step), xh=xh ^ (flip & 1), core=core ^ (flip >> 1))
+    beside = [{"xl": 1 - xl, "xh": xh}, {"xl": 1 - xl, "xh": 1 - xh}]
+    around = [{"y": y_at(1)}, {"y": y_at(3)}]
+    greet(z=up)
+    greet(z=down)
+    greet(**beside[0])
+    greet(core=1 - core)
+    for where in around + beside[1:]:
+        greet(**where)
+
+    def hello(kind, to):
+        for where in to:
+            pl.semaphore_signal(known.at[kind], inc=1, device_id=where, device_id_type=MESH)
+
+    def heard(kind, to):
+        pl.semaphore_wait(known.at[kind], len(to))
 
     mv[...] = jnp.zeros(mv.shape, mv.dtype)
     mv[0:10, :] = m1_ref[...]
     mv[16:26, :] = m2_ref[...]
     moms[side] = mv[...]
     loads[0].wait()
-    kbuf[z, xl] = kv[mine, :]
+    kbuf[z, pl.ds(2 * xl, 2)] = kv[mine, :].reshape(2, 32, 512)
     for i in range(1, 3):
         loads[i].wait()
-    pl.semaphore_wait(barrier, NZ - 1 + 7 + 12)
+    pl.semaphore_wait(barrier, 7)
 
     def copy_to(src, dst, send, recv, **where):
         return pltpu.make_async_remote_copy(
@@ -233,13 +243,13 @@
         back = step - 1
         return lax.rem(z + NZ - back, NZ) if way == 0 else lax.rem(z + back, NZ)
 
-    def key_copy(way, step, half):
-        part = kbuf.at[ring_block(way, step), half]
+    def key_copy(way, step, piece):
+        part = kbuf.at[ring_block(way, step), piece]
         return copy_to(
             part,
             part,
-            ag_send.at[way, step - 1, half],
-            ag_recv.at[way, step - 1, half],
+            ag_send.at[way, step - 1, piece],
+            ag_recv.at[way, step - 1, piece],
             z=up if way == 0 else down,
         )
 
@@ -253,23 +263,27 @@
             z=up if way == 0 else down,
         )
 
-    def part_copy(way, step, half):
+    def part_copy(way, step, piece):
         return copy_to(
-            rsend.at[way, step, half],
-            rrecv.at[way, step, half],
-            rs_send.at[way, step, half],
-            rs_recv.at[way, step, half],
+            rsend.at[way, step, piece],
+            rrecv.at[way, step, piece],
+            rs_send.at[way, step, piece],
+            rs_recv.at[way, step, piece],
             z=up if way == 0 else down,
         )
 
-    key_pair = pair_copy(kv.at[theirs], kbuf.at[z, xl], 0)
+    def key_pair(i):
+        rows = pl.ds(pl.multiple_of(64 * (1 - xl) + 32 * i, 32), 32)
+        return pair_copy(kv.at[rows], kbuf.at[z, 2 * xl + i], 5 * i)
+
     query_pair = pair_copy(qv.at[theirs], qst, 1)
     grad_pair = pair_copy(gsend.at[theirs], gst, 2)
     own_weight = wfull.at[core * NZ + z, :, lanes(y)]
     weight_pair = pair_copy(wv.at[:, lanes(y)], own_weight, 3)
-    key_pair.start()
-    for way in range(2):
-        key_copy(way, 1, xl).start()
+    for i in range(2):
+        key_pair(i).start()
+        for way in range(2):
+            key_copy(way, 1, 2 * xl + i).start()
 
     @pl.when(core == xl)
     def _():
@@ -277,6 +291,11 @@
         wfull[core * NZ + z, :, lanes(y)] = wv[:, lanes(y)]
 
     query_pair.start()
+    hello(0, around + beside[:1] + [{"core": 1 - core}])
+    for i in range(2):
+        key_pair(i).wait_recv()
+        for way in range(2):
+            key_copy(way, 1, 2 * (1 - xl) + i).start()
 
     for i in range(3, 9):
         loads[i].wait()
@@ -290,9 +309,6 @@
         gsend[:, cols] = (coeff_col * gv[:, cols].astype(jnp.float32)).astype(jnp.bfloat16)
     grad_pair.start()
 
-    key_pair.wait_recv()
-    for way in range(2):
-        key_copy(way, 1, 1 - xl).start()
 
     @pl.when(core != xl)
     def _():
@@ -312,16 +328,15 @@
     lrow[...] = jnp.zeros(lrow.shape, jnp.float32)
 
     def arrived(step):
-        for half in range(2):
+        for i in range(4):
+            piece = lax.rem(2 * xl + i, 4)
             for way in range(2):
                 if way == 1 and step == 8:
                     continue
-                key_copy(way, step, half).wait_recv()
+                key_copy(way, step, piece).wait_recv()
                 if step < 8 - way:
-                    key_copy(way, step + 1, half).start()
-        for way in range(2):
-            if way == 1 and step == 8:
-                continue
+                    key_copy(way, step + 1, piece).start()
+        for way in range(2 * (step < 8) + (step == 8)):
             weight_copy(way, step).wait_recv()
             if step < 8 - way:
                 weight_copy(way, step + 1).start()
@@ -408,18 +423,25 @@
         lax.fori_loop((first - 1) * KVH, last * KVH, score, 0)
 
     arrived(1)
+    heard(0, range(4))
+    hello(1, [{"core": 1 - core}])
     lax.fori_loop(0, 4, turn, 0)
     arrived(2)
+    heard(1, range(1))
+    hello(2, beside)
     lax.fori_loop(4, 8, turn, 0)
     xg[:, :, lanes(2 * y + core)] = xt[pl.ds(4 * core, 4), y]
     for copy in input_copies():
         copy.start()
     arrived(3)
-    for copy in moment_copies():
-        copy.start()
+    heard(2, range(2))
+    hello(3, beside)
     query_pair.wait_recv()
     spread(qh, qst, slice(None), 1 - xl)
     arrived(4)
+    heard(3, range(2))
+    for copy in moment_copies():
+        copy.start()
     scores(1, 2)
     arrived(5)
     scores(3, 4)
@@ -443,33 +465,43 @@
         across_y(step).start()
     scores(8, 8)
 
-    def part(t, which, slot):
-        def one(head, carry):
-            scale = jnp.exp2((mst[t - 1, head] - mrow[head]) * EXP_SCALE) / lrow[head]
-            p = eb[t - 1, head, pl.ds(which * 128, 128), :].astype(jnp.float32) * scale
-            pbuf[slot, :, lanes(head)] = jnp.dot(
-                p.astype(jnp.bfloat16), gh[head], preferred_element_type=jnp.float32
+    lrow[...] = 1.0 / lrow[...]
+
+    def parts(t, dst):
+        for head in range(KVH):
+            scale = jnp.exp2((mst[t - 1, head] - mrow[head]) * EXP_SCALE) * lrow[head]
+            p = (eb[t - 1, head].astype(jnp.float32) * scale).astype(jnp.bfloat16)
+            dst[:, head * HEAD : (head + 1) * HEAD] = jnp.dot(
+                p, gh[head], preferred_element_type=jnp.float32
             )
-            return carry
-
-        lax.fori_loop(0, KVH, one, 0)
-
-    def pass_on(way, step):
-        for half in range(2):
-            value = pbuf[way, half * 64 : (half + 1) * 64, :]
-            if step > 0:
-                part_copy(way, step - 1, half).wait_recv()
-                value = value + rrecv[way, step - 1, half].astype(jnp.float32)
-            rsend[way, step, half] = value.astype(jnp.bfloat16)
-            part_copy(way, step, half).start()
-
-    for step in range(8):
-        part(8 - step, 0 if step == 0 else 1, 0)
-        pass_on(0, step)
-        if step < 7:
-            part(7 - step, 0, 1)
-            pass_on(1, step)
-    part(8, 1, 0)
+
+    def pass_on(way, step, src, piece, first):
+        value = src[piece * 32 : (piece + 1) * 32, :]
+        if not first:
+            part_copy(way, step - 1, piece).wait_recv()
+            value = value + rrecv[way, step - 1, piece].astype(jnp.float32)
+        rsend[way, step, piece] = value.astype(jnp.bfloat16)
+        part_copy(way, step, piece).start()
+
+    parts(8, pbuf.at[0])
+    for piece in range(4):
+        pass_on(0, 0, pbuf.at[0, pl.ds(0, 128)], piece, True)
+    pown[...] = pbuf[0, 128:256, :]
+    parts(7, pbuf.at[1])
+    for piece in range(4):
+        pass_on(1, 0, pbuf.at[1, pl.ds(0, 128)], piece, True)
+    for piece in range(4):
+        pass_on(0, 1, pbuf.at[1, pl.ds(128, 128)], piece, False)
+
+    def ring_step(i, carry):
+        now = pbuf.at[lax.rem(i, 2)]
+        parts(8 - i, now)
+        for piece in range(4):
+            pass_on(1, i - 1, now.at[pl.ds(0, 128)], piece, False)
+            pass_on(0, i, now.at[pl.ds(128, 128)], piece, False)
+        return carry
+
+    lax.fori_loop(2, 8, ring_step, 0)
 
     for copy in moment_copies():
         copy.wait_recv()
@@ -478,21 +510,22 @@
         m2f[10 * s : 10 * s + 10, :] = moms[s, 16:26, :].astype(jnp.float32)
 
     value_pair = pair_copy(vsend, vrecv, 4)
-    for half in range(2):
-        part_copy(1, 6, half).wait_recv()
-        part_copy(0, 7, half).wait_recv()
-    vsend[...] = (
-        pbuf[0, theirs, :]
-        + rrecv[1, 6, 1 - xl].astype(jnp.float32)
-        + rrecv[0, 7, 1 - xl].astype(jnp.float32)
-    ).astype(jnp.bfloat16)
+    for piece in range(4):
+        part_copy(1, 6, piece).wait_recv()
+        part_copy(0, 7, piece).wait_recv()
+
+    def block_rows(half):
+        rows = pl.ds(2 * half, 2)
+        return (
+            pown[pl.ds(pl.multiple_of(64 * half, 64), 64), :]
+            + rrecv[1, 6, rows].reshape(64, 512).astype(jnp.float32)
+            + rrecv[0, 7, rows].reshape(64, 512).astype(jnp.float32)
+        ).astype(jnp.bfloat16)
+
+    vsend[...] = block_rows(1 - xl)
     value_pair.start()
     slot = 2 * y + core
-    vga[slot, mine, :] = (
-        pbuf[0, mine, :]
-        + rrecv[1, 6, xl].astype(jnp.float32)
-        + rrecv[0, 7, xl].astype(jnp.float32)
-    ).astype(jnp.bfloat16)
+    vga[slot, mine, :] = block_rows(xl)
     value_pair.wait_recv()
     vga[slot, theirs, :] = vrecv[...]
 
@@ -640,10 +673,10 @@
     for way in range(2):
         for step in range(8 - way):
             weight_copy(way, step + 1).wait_send()
-            for half in range(2):
-                key_copy(way, step + 1, half).wait_send()
-                part_copy(way, step, half).wait_send()
-    for copy in (key_pair, query_pair, grad_pair, value_pair):
+            for piece in range(4):
+                key_copy(way, step + 1, piece).wait_send()
+                part_copy(way, step, piece).wait_send()
+    for copy in (key_pair(0), key_pair(1), query_pair, grad_pair, value_pair):
         copy.wait_send()
 
     @pl.when(core == xl)
@@ -721,7 +754,7 @@
             buf(1, 32, kind=f32),
             buf(1, 32, kind=i32),
             buf(1, 32, kind=i32),
-            buf(NZ, 2, 64, 512),
+            buf(NZ, 4, 32, 512),
             buf(128, 2560),
             buf(64, 2560),
             buf(64, 2560),
@@ -731,9 +764,10 @@
             buf(8, KVH, 1, QB, kind=f32),
             buf(KVH, 1, QB, kind=f32),
             buf(KVH, 1, QB, kind=f32),
-            buf(2, 128, 512, kind=f32),
-            buf(2, 8, 2, 64, 512),
-            buf(2, 8, 2, 64, 512),
+            buf(2, 256, 512, kind=f32),
+            buf(128, 512, kind=f32),
+            buf(2, 8, 4, 32, 512),
+            buf(2, 8, 4, 32, 512),
             buf(64, 512),
             buf(64, 512),
             buf(8, 4, 160, 128),
@@ -753,12 +787,12 @@
             buf(160, 128),
             buf(4, 160, 128),
             dma((10,)),
-            dma((5,)),
-            dma((5,)),
-            dma((2, 8, 2)),
-            dma((2, 8, 2)),
-            dma((2, 8, 2)),
-            dma((2, 8, 2)),
+            dma((6,)),
+            dma((6,)),
+            dma((2, 8, 4)),
+            dma((2, 8, 4)),
+            dma((2, 8, 4)),
+            dma((2, 8, 4)),
             dma((8,)),
             dma((8,)),
             dma((2, 8)),
@@ -777,6 +811,7 @@
             dma,
             dma((4,)),
             dma((4,)),
+            pltpu.SemaphoreType.REGULAR((4,)),
         ],
         compiler_params=pltpu.CompilerParams(
             collective_id=0, has_side_effects=True, vmem_limit_bytes=60 * 1024 * 1024

time: 141 us -> 135 us (0.957)
  Pallas kernels: 136 us -> 129 us
    pallas_call x1, Pallas kernels: 136 us -> 129 us  [shards(): pl.pallas_call(kernel, out_shape=(jax.ShapeDtypeStruct((128, 5120), bf),...]
where the time goes in v3:
time: 135 us; the launch traced here: 134 us
  Pallas kernels  129 us (96%)
  local copies, waits for them, and re-layouts  4.39 us (3%)
    pallas_call x1, Pallas kernels, shards(): pl.pallas_call(kernel, out_shape=(jax.ShapeDtypeStruct((128, 5120), bf),...  129 us
    unnamed x10, local copies, waits for them, and re-layouts  4.39 us

profile of v3, /device:TPU:17, one launch (start us, length us, event | category | flops | bytes accessed | tf_op | source)
XLA Modules:
  0.0 134.5 jit_solution(11283343296853256284)
XLA Ops:
  0.6 129.4 %shard_map.147 = (bf16[128,5120]{1,0:T(8,128)(2,1)}, bf16[160,512]{1,0:T(8,128)(2,1)}, bf16[10,512]{1,0:T(8,128)(2,1)}, bf16[10,512]{1,0:T(8,128)(2,1)}) custom-call(bf16[128,5120]{1,0:T(8,128)(2,1)} %x_hbm.1, bf16[128,2560]{1,0:T(8,128)(2,1)} %q_hbm.1, bf16[128,512]{1,0:T(8,128)(2,1)} %k_hbm.1, bf16[128,2560]{1,0:T(8,128)(2,1)} %g_hbm.1, f32[1,128]{1,0:T(1,128)} %bitcast.5, ...), custom_call_target="tpu_custom_call" | custom-call | tf_op jit(solution)/shard_map/pallas_call | solution.py:736
  130.1 0.0 copy-start
  130.1 0.0 copy-start.2
  130.1 0.0 copy-start.1
  130.1 2.5 %copy.20 = bf16[128,5120]{1,0:T(8,128)(2,1)} copy(bf16[128,5120]{1,0:T(8,128)(2,1)} %get-tuple-element.8) | data formatting | bytes 2621440
  132.6 0.0 copy-done
  132.6 0.7 copy.21
  133.3 0.0 copy-done.2
  133.3 0.6 copy.22
  133.9 0.0 copy-done.1
  133.9 0.6 copy.23
Async XLA Ops:
  130.1 2.5 %copy-start = (bf16[160,512]{1,0:T(8,128)(2,1)S(1)}, bf16[160,512]{1,0:T(8,128)(2,1)}, u32[]{:S(2)}) copy-start(bf16[160,512]{1,0:T(8,128)(2,1)} %get-tuple-element.9) | copy-start | bytes 491524
  130.1 3.2 %copy-start.2 = (bf16[10,512]{1,0:T(8,128)(2,1)S(1)}, bf16[10,512]{1,0:T(8,128)(2,1)}, u32[]{:S(2)}) copy-start(bf16[10,512]{1,0:T(8,128)(2,1)} %get-tuple-element.10) | copy-start | bytes 30724
  130.1 3.8 %copy-start.1 = (bf16[10,512]{1,0:T(8,128)(2,1)S(1)}, bf16[10,512]{1,0:T(8,128)(2,1)}, u32[]{:S(2)}) copy-start(bf16[10,512]{1,0:T(8,128)(2,1)} %get-tuple-element.11) | copy-start | bytes 30724

commit v4 on v3

--- a/solution.py
+++ b/solution.py
@@ -292,10 +292,6 @@
 
     query_pair.start()
     hello(0, around + beside[:1] + [{"core": 1 - core}])
-    for i in range(2):
-        key_pair(i).wait_recv()
-        for way in range(2):
-            key_copy(way, 1, 2 * (1 - xl) + i).start()
 
     for i in range(3, 9):
         loads[i].wait()
@@ -308,6 +304,10 @@
         cols = slice(head * HEAD, (head + 1) * HEAD)
         gsend[:, cols] = (coeff_col * gv[:, cols].astype(jnp.float32)).astype(jnp.bfloat16)
     grad_pair.start()
+    for i in range(2):
+        key_pair(i).wait_recv()
+        for way in range(2):
+            key_copy(way, 1, 2 * (1 - xl) + i).start()
 
 
     @pl.when(core != xl)
@@ -317,36 +317,45 @@
     for way in range(2):
         weight_copy(way, 1).start()
 
-    def spread(dst, src, rows, half):
-        for head in range(KVH * PER):
-            at = pl.ds(pl.multiple_of(64 * half, 64) + (head % PER) * 128, 64)
-            dst[head // PER, at, :] = src[rows, head * HEAD : (head + 1) * HEAD]
-
-    spread(qh, qv, mine, xl)
-    spread(gh, gsend, mine, xl)
+    def spread(dst, src, rows, half, group):
+        for head in range(PER):
+            at = pl.ds(pl.multiple_of(64 * half, 64) + head * 128, 64)
+            col = (group * PER + head) * HEAD
+            dst[group, at, :] = src[rows, col : col + HEAD]
+
     mrow[...] = jnp.full(mrow.shape, LOW, jnp.float32)
     lrow[...] = jnp.zeros(lrow.shape, jnp.float32)
 
-    def arrived(step):
+    def arrived(step, work):
+        last = isinstance(step, int) and step == 8
         for i in range(4):
             piece = lax.rem(2 * xl + i, 4)
-            for way in range(2):
-                if way == 1 and step == 8:
-                    continue
-                key_copy(way, step, piece).wait_recv()
-                if step < 8 - way:
-                    key_copy(way, step + 1, piece).start()
-        for way in range(2 * (step < 8) + (step == 8)):
-            weight_copy(way, step).wait_recv()
-            if step < 8 - way:
-                weight_copy(way, step + 1).start()
+            key_copy(0, step, piece).wait_recv()
+            if last:
+                work(i)
+                continue
+            key_copy(0, step + 1, piece).start()
+            key_copy(1, step, piece).wait_recv()
+
+            @pl.when(step < 7)
+            def _():
+                key_copy(1, step + 1, piece).start()
+
+            work(i)
+        weight_copy(0, step).wait_recv()
+        if last:
+            return
+        weight_copy(0, step + 1).start()
+        weight_copy(1, step).wait_recv()
+
+        @pl.when(step < 7)
+        def _():
+            weight_copy(1, step + 1).start()
 
     loads[9].wait()
 
-    def turn(n, carry):
-        cols = pl.ds(pl.multiple_of(n * 640, 128), 640)
-        xt[n] = xv[:, cols].T.reshape(4, 160, 128)
-        return carry
+    def turn(n):
+        xt[n] = xv[:, n * 640 : (n + 1) * 640].T.reshape(4, 160, 128)
 
     def input_copies():
         copies = []
@@ -391,7 +400,7 @@
     in_block = lax.rem(row, 128)
     kpos_base = jnp.where(in_block < 64, in_block, in_block - 64 + 1024)
 
-    def score(index, carry):
+    def score(index):
         t = index // KVH + 1
         head = lax.rem(index, KVH)
         a = lax.rem(z + NZ - t, NZ)
@@ -417,41 +426,46 @@
         mrow[head] = top
         mst[t - 1, head] = top
         eb[t - 1, head] = e.astype(jnp.bfloat16)
-        return carry
-
-    def scores(first, last):
-        lax.fori_loop((first - 1) * KVH, last * KVH, score, 0)
-
-    arrived(1)
+
+    arrived(1, lambda i: spread(qh, qv, mine, xl, i))
     heard(0, range(4))
     hello(1, [{"core": 1 - core}])
-    lax.fori_loop(0, 4, turn, 0)
-    arrived(2)
+    arrived(2, lambda i: turn(i))
     heard(1, range(1))
     hello(2, beside)
-    lax.fori_loop(4, 8, turn, 0)
-    xg[:, :, lanes(2 * y + core)] = xt[pl.ds(4 * core, 4), y]
+    arrived(3, lambda i: turn(4 + i))
+    heard(2, range(2))
+    hello(3, beside)
     for copy in input_copies():
         copy.start()
-    arrived(3)
-    heard(2, range(2))
-    hello(3, beside)
     query_pair.wait_recv()
-    spread(qh, qst, slice(None), 1 - xl)
-    arrived(4)
+
+    def second_half(i):
+        spread(qh, qst, slice(None), 1 - xl, i)
+        spread(gh, gsend, mine, xl, i)
+
+    arrived(4, second_half)
     heard(3, range(2))
     for copy in moment_copies():
         copy.start()
-    scores(1, 2)
-    arrived(5)
-    scores(3, 4)
-    arrived(6)
-    scores(5, 5)
-    arrived(7)
-    scores(6, 7)
+
+    def key_step(step, carry):
+        def work(i):
+            for unit in range(2):
+                score((step - 5) * 8 + i * 2 + unit)
+
+        arrived(step, work)
+        return carry
+
+    lax.fori_loop(5, 8, key_step, 0)
+    xg[:, :, lanes(2 * y + core)] = xt[pl.ds(4 * core, 4), y]
     grad_pair.wait_recv()
-    spread(gh, gst, slice(None), 1 - xl)
-    arrived(8)
+
+    def last_step(i):
+        score(24 + i)
+        spread(gh, gst, slice(None), 1 - xl, i)
+
+    arrived(8, last_step)
 
     def across_y(step):
         part = wfull.at[pl.ds(NZ * core, NZ), :, lanes(y)]
@@ -463,17 +477,17 @@
 
     for step in range(1, 4):
         across_y(step).start()
-    scores(8, 8)
+    for head in range(KVH):
+        score(28 + head)
 
     lrow[...] = 1.0 / lrow[...]
 
-    def parts(t, dst):
-        for head in range(KVH):
-            scale = jnp.exp2((mst[t - 1, head] - mrow[head]) * EXP_SCALE) * lrow[head]
-            p = (eb[t - 1, head].astype(jnp.float32) * scale).astype(jnp.bfloat16)
-            dst[:, head * HEAD : (head + 1) * HEAD] = jnp.dot(
-                p, gh[head], preferred_element_type=jnp.float32
-            )
+    def parts(t, dst, head):
+        scale = jnp.exp2((mst[t - 1, head] - mrow[head]) * EXP_SCALE) * lrow[head]
+        p = (eb[t - 1, head].astype(jnp.float32) * scale).astype(jnp.bfloat16)
+        dst[:, head * HEAD : (head + 1) * HEAD] = jnp.dot(
+            p, gh[head], preferred_element_type=jnp.float32
+        )
 
     def pass_on(way, step, src, piece, first):
         value = src[piece * 32 : (piece + 1) * 32, :]
@@ -483,25 +497,33 @@
         rsend[way, step, piece] = value.astype(jnp.bfloat16)
         part_copy(way, step, piece).start()
 
-    parts(8, pbuf.at[0])
+    for head in range(KVH):
+        parts(8, pbuf.at[0], head)
     for piece in range(4):
         pass_on(0, 0, pbuf.at[0, pl.ds(0, 128)], piece, True)
     pown[...] = pbuf[0, 128:256, :]
-    parts(7, pbuf.at[1])
+    for head in range(KVH):
+        parts(7, pbuf.at[1], head)
     for piece in range(4):
         pass_on(1, 0, pbuf.at[1, pl.ds(0, 128)], piece, True)
+    for head in range(KVH):
+        parts(6, pbuf.at[0], head)
     for piece in range(4):
         pass_on(0, 1, pbuf.at[1, pl.ds(128, 128)], piece, False)
 
     def ring_step(i, carry):
         now = pbuf.at[lax.rem(i, 2)]
-        parts(8 - i, now)
+        later = pbuf.at[1 - lax.rem(i, 2)]
         for piece in range(4):
             pass_on(1, i - 1, now.at[pl.ds(0, 128)], piece, False)
             pass_on(0, i, now.at[pl.ds(128, 128)], piece, False)
+            parts(7 - i, later, piece)
         return carry
 
-    lax.fori_loop(2, 8, ring_step, 0)
+    lax.fori_loop(2, 7, ring_step, 0)
+    for piece in range(4):
+        pass_on(1, 6, pbuf.at[1, pl.ds(0, 128)], piece, False)
+        pass_on(0, 7, pbuf.at[1, pl.ds(128, 128)], piece, False)
 
     for copy in moment_copies():
         copy.wait_recv()
@@ -561,21 +583,24 @@
         values_core(step).wait_recv()
         add_inputs(step, False)
 
-    def sum_x(step):
+    def sum_x(step, half):
         at = lax.rem(x + step, 4)
+        rows = pl.ds(320 * half, 320)
         return copy_to(
-            xs.at[step - 1],
-            xr.at[step - 1],
-            xs_send.at[step - 1],
-            xs_recv.at[step - 1],
+            xs.at[step - 1, rows],
+            xr.at[step - 1, rows],
+            xs_send.at[step - 1, half],
+            xs_recv.at[step - 1, half],
             xl=lax.rem(at, 2),
             xh=at // 2,
         )
 
-    for step in (2, 1, 3):
-        at = lax.rem(x + step, 4)
-        xs[step - 1] = acc[:, lanes(at)].astype(jnp.bfloat16)
-        sum_x(step).start()
+    for half in range(2):
+        rows = pl.ds(320 * half, 320)
+        for step in (2, 1, 3):
+            at = lax.rem(x + step, 4)
+            xs[step - 1, rows] = acc[rows, lanes(at)].astype(jnp.bfloat16)
+            sum_x(step, half).start()
 
     across_core().wait_recv()
 
@@ -588,24 +613,24 @@
 
     lax.fori_loop(0, 8, grad_tile, 0)
 
-    for step in (1, 3, 2):
-        sum_x(step).wait_recv()
-    total = acc[:, lanes(x)]
-    for step in range(3):
-        total = total + xr[step].astype(jnp.float32)
-    zsum[...] = total.reshape(4, 160, 128)
-    zs[...] = zsum[...].astype(jnp.bfloat16)
-
     def sum_z(j):
         at = 4 * j + y
         far = lax.rem(z - at + NZ, NZ)
         return copy_to(zs.at[j], zr.at[far], zs_send.at[j], zs_recv.at[far], z=at)
 
-    for j in range(4):
-
-        @pl.when(z != 4 * j + y)
-        def _(j=j):
-            sum_z(j).start()
+    for half in range(2):
+        rows = pl.ds(320 * half, 320)
+        total = acc[rows, lanes(x)]
+        for step in (1, 3, 2):
+            sum_x(step, half).wait_recv()
+            total = total + xr[step - 1, rows].astype(jnp.float32)
+        zsum[2 * half : 2 * half + 2] = total.reshape(2, 160, 128)
+        zs[2 * half : 2 * half + 2] = total.reshape(2, 160, 128).astype(jnp.bfloat16)
+        for j in range(2 * half, 2 * half + 2):
+
+            @pl.when(z != 4 * j + y)
+            def _(j=j):
+                sum_z(j).start()
 
     root = lax.rem(z, 4) == y
 
@@ -691,7 +716,8 @@
         across_y(step).wait_send()
         values_y(step).wait_send()
         values_core(step).wait_send()
-        sum_x(step).wait_send()
+        for half in range(2):
+            sum_x(step, half).wait_send()
     for j in range(4):
 
         @pl.when(z != 4 * j + y)
@@ -803,8 +829,8 @@
             dma((16,)),
             dma((8,)),
             dma((8,)),
-            dma((3,)),
-            dma((3,)),
+            dma((3, 2)),
+            dma((3, 2)),
             dma((4,)),
             dma((16,)),
             dma((3,)),

time: 135 us -> 128 us (0.948)
  the two profiles are of different devices: /device:TPU:17 before, /device:TPU:33 now
where the time goes in v4:
time: 128 us
  Pallas kernels  123 us (96%)
  local copies, waits for them, and re-layouts  4.39 us (3%)
    pallas_call x1, Pallas kernels, shards(): pl.pallas_call(kernel, out_shape=(jax.ShapeDtypeStruct((128, 5120), bf),...  123 us
    unnamed x10, local copies, waits for them, and re-layouts  4.39 us

profile of v4, /device:TPU:33, one launch (start us, length us, event | category | flops | bytes accessed | tf_op | source)
XLA Modules:
  0.0 127.9 jit_solution(14520628105689889856)
XLA Ops:
  0.6 122.8 %shard_map.147 = (bf16[128,5120]{1,0:T(8,128)(2,1)}, bf16[160,512]{1,0:T(8,128)(2,1)}, bf16[10,512]{1,0:T(8,128)(2,1)}, bf16[10,512]{1,0:T(8,128)(2,1)}) custom-call(bf16[128,5120]{1,0:T(8,128)(2,1)} %x_hbm.1, bf16[128,2560]{1,0:T(8,128)(2,1)} %q_hbm.1, bf16[128,512]{1,0:T(8,128)(2,1)} %k_hbm.1, bf16[128,2560]{1,0:T(8,128)(2,1)} %g_hbm.1, f32[1,128]{1,0:T(1,128)} %bitcast.5, ...), custom_call_target="tpu_custom_call" | custom-call | tf_op jit(solution)/shard_map/pallas_call | solution.py:762
  123.5 0.0 copy-start
  123.5 0.0 copy-start.2
  123.5 0.0 copy-start.1
  123.5 2.5 %copy.20 = bf16[128,5120]{1,0:T(8,128)(2,1)} copy(bf16[128,5120]{1,0:T(8,128)(2,1)} %get-tuple-element.8) | data formatting | bytes 2621440
  126.0 0.0 copy-done
  126.0 0.7 copy.21
  126.7 0.0 copy-done.2
  126.7 0.6 copy.22
  127.3 0.0 copy-done.1
  127.3 0.6 copy.23
Async XLA Ops:
  123.5 2.5 %copy-start = (bf16[160,512]{1,0:T(8,128)(2,1)S(1)}, bf16[160,512]{1,0:T(8,128)(2,1)}, u32[]{:S(2)}) copy-start(bf16[160,512]{1,0:T(8,128)(2,1)} %get-tuple-element.9) | copy-start | bytes 491524
  123.5 3.2 %copy-start.2 = (bf16[10,512]{1,0:T(8,128)(2,1)S(1)}, bf16[10,512]{1,0:T(8,128)(2,1)}, u32[]{:S(2)}) copy-start(bf16[10,512]{1,0:T(8,128)(2,1)} %get-tuple-element.10) | copy-start | bytes 30724
  123.5 3.8 %copy-start.1 = (bf16[10,512]{1,0:T(8,128)(2,1)S(1)}, bf16[10,512]{1,0:T(8,128)(2,1)}, u32[]{:S(2)}) copy-start(bf16[10,512]{1,0:T(8,128)(2,1)} %get-tuple-element.11) | copy-start | bytes 30724

commit v5 on v4

--- a/solution.py
+++ b/solution.py
@@ -113,7 +113,7 @@
     rsend,
     rrecv,
     vsend,
-    vrecv,
+    igv,
     xt,
     xg,
     wfull,
@@ -192,9 +192,7 @@
             )
         )
     ]
-    for load in loads:
-        load.start()
-
+    loads[0].start()
     barrier = pltpu.get_barrier_semaphore()
 
     def greet(**where):
@@ -216,14 +214,10 @@
     def heard(kind, to):
         pl.semaphore_wait(known.at[kind], len(to))
 
-    mv[...] = jnp.zeros(mv.shape, mv.dtype)
-    mv[0:10, :] = m1_ref[...]
-    mv[16:26, :] = m2_ref[...]
-    moms[side] = mv[...]
+    for load in loads[1:]:
+        load.start()
     loads[0].wait()
     kbuf[z, pl.ds(2 * xl, 2)] = kv[mine, :].reshape(2, 32, 512)
-    for i in range(1, 3):
-        loads[i].wait()
     pl.semaphore_wait(barrier, 7)
 
     def copy_to(src, dst, send, recv, **where):
@@ -284,6 +278,8 @@
         key_pair(i).start()
         for way in range(2):
             key_copy(way, 1, 2 * xl + i).start()
+    for i in range(1, 3):
+        loads[i].wait()
 
     @pl.when(core == xl)
     def _():
@@ -393,6 +389,11 @@
                     )
         return copies
 
+    mv[...] = jnp.zeros(mv.shape, mv.dtype)
+    mv[0:10, :] = m1_ref[...]
+    mv[16:26, :] = m2_ref[...]
+    moms[side] = mv[...]
+
     row = lax.broadcasted_iota(jnp.int32, (256, 1), 0)
     lane = lax.broadcasted_iota(jnp.int32, (1, QB), 1)
     in_head = lax.rem(lane, 128)
@@ -490,7 +491,8 @@
         )
 
     def pass_on(way, step, src, piece, first):
-        value = src[piece * 32 : (piece + 1) * 32, :]
+        piece = lax.rem(piece + 2 * (1 - xl), 4)
+        value = src[pl.ds(pl.multiple_of(piece * 32, 32), 32), :]
         if not first:
             part_copy(way, step - 1, piece).wait_recv()
             value = value + rrecv[way, step - 1, piece].astype(jnp.float32)
@@ -525,18 +527,13 @@
         pass_on(1, 6, pbuf.at[1, pl.ds(0, 128)], piece, False)
         pass_on(0, 7, pbuf.at[1, pl.ds(128, 128)], piece, False)
 
-    for copy in moment_copies():
-        copy.wait_recv()
-    for s in range(16):
-        m1f[10 * s : 10 * s + 10, :] = moms[s, 0:10, :].astype(jnp.float32)
-        m2f[10 * s : 10 * s + 10, :] = moms[s, 16:26, :].astype(jnp.float32)
-
-    value_pair = pair_copy(vsend, vrecv, 4)
-    for piece in range(4):
-        part_copy(1, 6, piece).wait_recv()
-        part_copy(0, 7, piece).wait_recv()
+    slot = 2 * y + core
+    value_pair = pair_copy(vsend, vga.at[slot, mine], 4)
 
     def block_rows(half):
+        for i in range(2):
+            part_copy(1, 6, 2 * half + i).wait_recv()
+            part_copy(0, 7, 2 * half + i).wait_recv()
         rows = pl.ds(2 * half, 2)
         return (
             pown[pl.ds(pl.multiple_of(64 * half, 64), 64), :]
@@ -544,29 +541,34 @@
             + rrecv[0, 7, rows].reshape(64, 512).astype(jnp.float32)
         ).astype(jnp.bfloat16)
 
+    def value_part(at, part):
+        return vga.at[at, theirs if part else mine]
+
+    def values_y(step, part):
+        rows = value_part(slot, part)
+        return copy_to(
+            rows, rows, va_send.at[step, part], va_recv.at[step, part], y=y_at(step)
+        )
+
+    def values_core(step, part):
+        rows = value_part(2 * lax.rem(y + 4 - step, 4) + core, part)
+        return copy_to(
+            rows, rows, va_send.at[4 + step, part], va_recv.at[4 + step, part], core=1 - core
+        )
+
     vsend[...] = block_rows(1 - xl)
     value_pair.start()
-    slot = 2 * y + core
     vga[slot, mine, :] = block_rows(xl)
+    for step in (2, 1, 3):
+        values_y(step, 0).start()
+    values_core(0, 0).start()
     value_pair.wait_recv()
-    vga[slot, theirs, :] = vrecv[...]
-
-    def values_y(step):
-        return copy_to(vga.at[slot], vga.at[slot], va_send.at[step], va_recv.at[step], y=y_at(step))
-
-    def values_core(step):
-        part = vga.at[2 * lax.rem(y + 4 - step, 4) + core]
-        return copy_to(part, part, va_send.at[4 + step], va_recv.at[4 + step], core=1 - core)
-
     for step in (2, 1, 3):
-        values_y(step).start()
-    values_core(0).start()
+        values_y(step, 1).start()
+    values_core(0, 1).start()
 
     for copy in input_copies():
         copy.wait_recv()
-    for step in range(1, 4):
-        across_y(step).wait_recv()
-    across_core().start()
 
     def add_inputs(step, first):
         at = lax.rem(y + 4 - step, 4)
@@ -575,12 +577,17 @@
         value = jnp.dot(a, b, preferred_element_type=jnp.float32)
         acc[...] = value if first else acc[...] + value
 
-    values_core(0).wait_recv()
+    for step in (1, 3, 2):
+        values_y(step, 0).wait_recv()
+        values_core(step, 0).start()
+    for part in range(2):
+        values_core(0, part).wait_recv()
     add_inputs(0, True)
     for step in (1, 3, 2):
-        values_y(step).wait_recv()
-        values_core(step).start()
-        values_core(step).wait_recv()
+        values_y(step, 1).wait_recv()
+        values_core(step, 1).start()
+        for part in range(2):
+            values_core(step, part).wait_recv()
         add_inputs(step, False)
 
     def sum_x(step, half):
@@ -602,16 +609,27 @@
             xs[step - 1, rows] = acc[rows, lanes(at)].astype(jnp.bfloat16)
             sum_x(step, half).start()
 
-    across_core().wait_recv()
-
-    def grad_tile(n, carry):
-        w = wfull[pl.ds(4 * n, 4)].reshape(640, 512)
-        ig_ref[:, pl.ds(pl.multiple_of(n * 640, 128), 640)] = lax.dot_general(
-            vga[slot], w, (((1,), (1,)), ((), ())), preferred_element_type=jnp.float32
-        ).astype(jnp.bfloat16)
-        return carry
-
-    lax.fori_loop(0, 8, grad_tile, 0)
+    for step in range(1, 4):
+        across_y(step).wait_recv()
+    across_core().start()
+
+    for copy in moment_copies():
+        copy.wait_recv()
+    for s in range(16):
+        m1f[10 * s : 10 * s + 10, :] = moms[s, 0:10, :].astype(jnp.float32)
+        m2f[10 * s : 10 * s + 10, :] = moms[s, 16:26, :].astype(jnp.float32)
+
+    for way in range(2):
+        for step in range(8 - way):
+            weight_copy(way, step + 1).wait_send()
+            for piece in range(4):
+                key_copy(way, step + 1, piece).wait_send()
+    for copy in [key_pair(0), key_pair(1), query_pair, grad_pair] + input_copies():
+        copy.wait_send()
+
+    @pl.when(core == xl)
+    def _():
+        weight_pair.wait_send()
 
     def sum_z(j):
         at = 4 * j + y
@@ -632,6 +650,38 @@
             def _(j=j):
                 sum_z(j).start()
 
+    across_core().wait_recv()
+
+    def grad_tile(n, carry):
+        w = wfull[pl.ds(4 * n, 4)].reshape(640, 512)
+        igv[:, pl.ds(pl.multiple_of(n * 640, 128), 640)] = lax.dot_general(
+            vga[slot], w, (((1,), (1,)), ((), ())), preferred_element_type=jnp.float32
+        ).astype(jnp.bfloat16)
+        return carry
+
+    lax.fori_loop(0, 8, grad_tile, 0)
+    grad_out = [
+        pltpu.make_async_copy(igv.at[pl.ds(32 * i, 32)], ig_ref.at[pl.ds(32 * i, 32)], load_sem.at[i])
+        for i in range(4)
+    ]
+    for out in grad_out:
+        out.start()
+    for way in range(2):
+        for step in range(8 - way):
+            for piece in range(4):
+                part_copy(way, step, piece).wait_send()
+    value_pair.wait_send()
+    for copy in moment_copies():
+        copy.wait_send()
+    for step in range(1, 4):
+        across_y(step).wait_send()
+        for half in range(2):
+            values_y(step, half).wait_send()
+            sum_x(step, half).wait_send()
+    for step in range(4):
+        for part in range(2):
+            values_core(step, part).wait_send()
+
     root = lax.rem(z, 4) == y
 
     def spread_y(step):
@@ -677,7 +727,6 @@
         def _(at=at):
             copy_to(gy, gf.at[at], gf_send.at[0], gf_recv.at[at], core=1 - core).wait_recv()
 
-    for at in range(4):
         cols = slice(at * 128, (at + 1) * 128)
         new, first, second = adam_rows(
             wv[:, cols].astype(jnp.float32),
@@ -695,29 +744,9 @@
             nf_ref[...] = m1f[10 * s : 10 * s + 10, :].astype(jnp.bfloat16)
             ns_ref[...] = m2f[10 * s : 10 * s + 10, :].astype(jnp.bfloat16)
 
-    for way in range(2):
-        for step in range(8 - way):
-            weight_copy(way, step + 1).wait_send()
-            for piece in range(4):
-                key_copy(way, step + 1, piece).wait_send()
-                part_copy(way, step, piece).wait_send()
-    for copy in (key_pair(0), key_pair(1), query_pair, grad_pair, value_pair):
-        copy.wait_send()
-
-    @pl.when(core == xl)
-    def _():
-        weight_pair.wait_send()
-
-    for copy in input_copies() + moment_copies():
-        copy.wait_send()
     across_core().wait_send()
-    values_core(0).wait_send()
-    for step in range(1, 4):
-        across_y(step).wait_send()
-        values_y(step).wait_send()
-        values_core(step).wait_send()
-        for half in range(2):
-            sum_x(step, half).wait_send()
+    for out in grad_out:
+        out.wait()
     for j in range(4):
 
         @pl.when(z != 4 * j + y)
@@ -759,7 +788,7 @@
     def buf(*shape, kind=bf):
         return pltpu.VMEM(shape, kind)
 
-    return pl.pallas_call(
+    outs = pl.pallas_call(
         kernel,
         out_shape=(
             jax.ShapeDtypeStruct((128, 5120), bf),
@@ -768,7 +797,7 @@
             jax.ShapeDtypeStruct((10, 512), bf),
         ),
         in_specs=[hbm] * 10 + [vmem] * 2,
-        out_specs=(vmem,) * 4,
+        out_specs=(hbm, vmem, vmem, vmem),
         scratch_shapes=[
             buf(128, 2560),
             buf(128, 2560),
@@ -795,7 +824,7 @@
             buf(2, 8, 4, 32, 512),
             buf(2, 8, 4, 32, 512),
             buf(64, 512),
-            buf(64, 512),
+            buf(128, 5120),
             buf(8, 4, 160, 128),
             buf(4, 160, 1024),
             buf(32, 160, 512),
@@ -827,8 +856,8 @@
             dma((4,)),
             dma((16,)),
             dma((16,)),
-            dma((8,)),
-            dma((8,)),
+            dma((8, 2)),
+            dma((8, 2)),
             dma((3, 2)),
             dma((3, 2)),
             dma((4,)),
@@ -856,6 +885,39 @@
         first_moment,
         second_moment,
     )
+    return pl.pallas_call(
+        hand_over,
+        out_shape=[jax.ShapeDtypeStruct(o.shape, o.dtype) for o in outs],
+        in_specs=[hbm, hbm, vmem, vmem],
+        out_specs=[hbm, hbm, vmem, vmem],
+        scratch_shapes=[buf(128, 5120), buf(160, 512), dma((5,)), dma((5,))],
+        compiler_params=pltpu.CompilerParams(vmem_limit_bytes=60 * 1024 * 1024),
+    )(*outs)
+
+
+def hand_over(
+    ig_in, np_in, nf_in, ns_in, ig_out, np_out, nf_out, ns_out, ig_mid, np_mid, sem_in, sem_out
+):
+    def pieces(ig_from, np_from, ig_to, np_to, sem):
+        copies = [pltpu.make_async_copy(np_from, np_to, sem.at[0])]
+        for i in range(4):
+            rows = pl.ds(32 * i, 32)
+            copies.append(
+                pltpu.make_async_copy(ig_from.at[rows], ig_to.at[rows], sem.at[i + 1])
+            )
+        return copies
+
+    fetched = pieces(ig_in, np_in, ig_mid, np_mid, sem_in)
+    stored = pieces(ig_mid, np_mid, ig_out, np_out, sem_out)
+    for copy in fetched:
+        copy.start()
+    nf_out[...] = nf_in[...]
+    ns_out[...] = ns_in[...]
+    for before, after in zip(fetched, stored):
+        before.wait()
+        after.start()
+    for copy in stored:
+        copy.wait()
 
 
 def solution(mesh):

time: 128 us -> 124 us (0.969)
  local copies, waits for them, and re-layouts: 4.39 us -> 0 us
    unnamed x10 -> x0, local copies, waits for them, and re-layouts: 4.39 us -> none
    pallas_call x0 -> x1, Pallas kernels: none -> 3.54 us  [shards(): pl.pallas_call(hand_over, out_shape=[jax.ShapeDtypeStruct(o.shape, o.dtyp...]
    pallas_call x1, Pallas kernels: 123 us -> 119 us  [shards(): pl.pallas_call(kernel, out_shape=(jax.ShapeDtypeStruct((128, 5120), bf),...]
where the time goes in v5:
time: 124 us
  Pallas kernels  123 us (99%)
    pallas_call x1, Pallas kernels, shards(): pl.pallas_call(kernel, out_shape=(jax.ShapeDtypeStruct((128, 5120), bf),...  119 us
    pallas_call x1, Pallas kernels, shards(): pl.pallas_call(hand_over, out_shape=[jax.ShapeDtypeStruct(o.shape, o.dtyp...  3.54 us

profile of v5, /device:TPU:33, one launch (start us, length us, event | category | flops | bytes accessed | tf_op | source)
XLA Modules:
  0.0 123.5 jit_solution(4375036487310317764)
XLA Ops:
  0.6 119.3 %shard_map.147 = (bf16[128,5120]{1,0:T(8,128)(2,1)}, bf16[160,512]{1,0:T(8,128)(2,1)}, bf16[10,512]{1,0:T(8,128)(2,1)}, bf16[10,512]{1,0:T(8,128)(2,1)}) custom-call(bf16[128,5120]{1,0:T(8,128)(2,1)} %x_hbm.1, bf16[128,2560]{1,0:T(8,128)(2,1)} %q_hbm.1, bf16[128,512]{1,0:T(8,128)(2,1)} %k_hbm.1, bf16[128,2560]{1,0:T(8,128)(2,1)} %g_hbm.1, f32[1,128]{1,0:T(1,128)} %bitcast.5, ...), custom_call_target="tpu_custom_call" | custom-call | tf_op jit(solution)/shard_map/pallas_call | solution.py:791
  120.0 3.5 %shard_map.148 = (bf16[128,5120]{1,0:T(8,128)(2,1)}, bf16[160,512]{1,0:T(8,128)(2,1)}, bf16[10,512]{1,0:T(8,128)(2,1)}, bf16[10,512]{1,0:T(8,128)(2,1)}) custom-call(bf16[128,5120]{1,0:T(8,128)(2,1)} %get-tuple-element.8.ig_in, bf16[160,512]{1,0:T(8,128)(2,1)} %get-tuple-element.9.np_in, bf16[10,512]{1,0:T(8,128)(2,1)} %get-tuple-element.10.nf_in, ...), custom_call_target="tpu_custom_call" | custom-call | tf_op jit(solution)/shard_map/pallas_call | solution.py:888

commit v6 on v5

--- a/solution.py
+++ b/solution.py
@@ -619,6 +619,15 @@
         m1f[10 * s : 10 * s + 10, :] = moms[s, 0:10, :].astype(jnp.float32)
         m2f[10 * s : 10 * s + 10, :] = moms[s, 16:26, :].astype(jnp.float32)
 
+    def grad_tile(n, carry):
+        w = wfull[pl.ds(4 * n, 4)].reshape(640, 512)
+        igv[:, pl.ds(pl.multiple_of(n * 640, 128), 640)] = lax.dot_general(
+            vga[slot], w, (((1,), (1,)), ((), ())), preferred_element_type=jnp.float32
+        ).astype(jnp.bfloat16)
+        return carry
+
+    lax.fori_loop(4 * core, 4 * core + 4, grad_tile, 0)
+
     for way in range(2):
         for step in range(8 - way):
             weight_copy(way, step + 1).wait_send()
@@ -651,21 +660,52 @@
                 sum_z(j).start()
 
     across_core().wait_recv()
-
-    def grad_tile(n, carry):
-        w = wfull[pl.ds(4 * n, 4)].reshape(640, 512)
-        igv[:, pl.ds(pl.multiple_of(n * 640, 128), 640)] = lax.dot_general(
-            vga[slot], w, (((1,), (1,)), ((), ())), preferred_element_type=jnp.float32
-        ).astype(jnp.bfloat16)
-        return carry
-
-    lax.fori_loop(0, 8, grad_tile, 0)
+    lax.fori_loop(4 * (1 - core), 4 * (1 - core) + 4, grad_tile, 0)
     grad_out = [
         pltpu.make_async_copy(igv.at[pl.ds(32 * i, 32)], ig_ref.at[pl.ds(32 * i, 32)], load_sem.at[i])
         for i in range(4)
     ]
     for out in grad_out:
         out.start()
+    root = lax.rem(z, 4) == y
+
+    def spread_y(step):
+        return copy_to(gy, gy, gy_send.at[step - 1], gy_recv, y=y_at(step))
+
+    @pl.when(root)
+    def _():
+        total = zsum[z // 4]
+        for far in range(1, NZ):
+            copy_to(zs.at[0], zr.at[far], zs_send.at[0], zs_recv.at[far], z=up).wait_recv()
+            total = total + zr[far].astype(jnp.float32)
+        gy[...] = total.astype(jnp.bfloat16)
+        for step in range(1, 4):
+            spread_y(step).start()
+
+    @pl.when(jnp.logical_not(root))
+    def _():
+        spread_y(1).wait_recv()
+
+    def spread_x(to_xh, to_core):
+        k = to_xh * 2 + to_core
+        return copy_to(
+            gy, gf.at[x], gf_send.at[k], gf_recv.at[x], xl=core, xh=to_xh, core=to_core
+        )
+
+    def is_self(to_xh, to_core):
+        return (xl == core) & (xh == to_xh) & (core == to_core)
+
+    for to_xh in range(2):
+        for to_core in range(2):
+
+            @pl.when(jnp.logical_not(is_self(to_xh, to_core)))
+            def _(to_xh=to_xh, to_core=to_core):
+                spread_x(to_xh, to_core).start()
+
+    @pl.when(xl == core)
+    def _():
+        gf[x] = gy[...]
+
     for way in range(2):
         for step in range(8 - way):
             for piece in range(4):
@@ -681,45 +721,6 @@
     for step in range(4):
         for part in range(2):
             values_core(step, part).wait_send()
-
-    root = lax.rem(z, 4) == y
-
-    def spread_y(step):
-        return copy_to(gy, gy, gy_send.at[step - 1], gy_recv, y=y_at(step))
-
-    @pl.when(root)
-    def _():
-        total = zsum[z // 4]
-        for far in range(1, NZ):
-            copy_to(zs.at[0], zr.at[far], zs_send.at[0], zs_recv.at[far], z=up).wait_recv()
-            total = total + zr[far].astype(jnp.float32)
-        gy[...] = total.astype(jnp.bfloat16)
-        for step in range(1, 4):
-            spread_y(step).start()
-
-    @pl.when(jnp.logical_not(root))
-    def _():
-        spread_y(1).wait_recv()
-
-    def spread_x(to_xh, to_core):
-        k = to_xh * 2 + to_core
-        return copy_to(
-            gy, gf.at[x], gf_send.at[k], gf_recv.at[x], xl=core, xh=to_xh, core=to_core
-        )
-
-    def is_self(to_xh, to_core):
-        return (xl == core) & (xh == to_xh) & (core == to_core)
-
-    for to_xh in range(2):
-        for to_core in range(2):
-
-            @pl.when(jnp.logical_not(is_self(to_xh, to_core)))
-            def _(to_xh=to_xh, to_core=to_core):
-                spread_x(to_xh, to_core).start()
-
-    @pl.when(xl == core)
-    def _():
-        gf[x] = gy[...]
 
     for at in range(4):
 
@@ -888,36 +889,17 @@
     return pl.pallas_call(
         hand_over,
         out_shape=[jax.ShapeDtypeStruct(o.shape, o.dtype) for o in outs],
-        in_specs=[hbm, hbm, vmem, vmem],
-        out_specs=[hbm, hbm, vmem, vmem],
-        scratch_shapes=[buf(128, 5120), buf(160, 512), dma((5,)), dma((5,))],
+        in_specs=[vmem] * 4,
+        out_specs=[vmem] * 4,
         compiler_params=pltpu.CompilerParams(vmem_limit_bytes=60 * 1024 * 1024),
     )(*outs)
 
 
-def hand_over(
-    ig_in, np_in, nf_in, ns_in, ig_out, np_out, nf_out, ns_out, ig_mid, np_mid, sem_in, sem_out
-):
-    def pieces(ig_from, np_from, ig_to, np_to, sem):
-        copies = [pltpu.make_async_copy(np_from, np_to, sem.at[0])]
-        for i in range(4):
-            rows = pl.ds(32 * i, 32)
-            copies.append(
-                pltpu.make_async_copy(ig_from.at[rows], ig_to.at[rows], sem.at[i + 1])
-            )
-        return copies
-
-    fetched = pieces(ig_in, np_in, ig_mid, np_mid, sem_in)
-    stored = pieces(ig_mid, np_mid, ig_out, np_out, sem_out)
-    for copy in fetched:
-        copy.start()
+def hand_over(ig_in, np_in, nf_in, ns_in, ig_out, np_out, nf_out, ns_out):
+    ig_out[...] = ig_in[...]
+    np_out[...] = np_in[...]
     nf_out[...] = nf_in[...]
     ns_out[...] = ns_in[...]
-    for before, after in zip(fetched, stored):
-        before.wait()
-        after.start()
-    for copy in stored:
-        copy.wait()
 
 
 def solution(mesh):

time: 124 us -> 123 us (level)
  no operation moved by 1% of the time
where the time goes in v6:
time: 123 us
  Pallas kernels  122 us (99%)
    pallas_call x1, Pallas kernels, shards(): pl.pallas_call(kernel, out_shape=(jax.ShapeDtypeStruct((128, 5120), bf),...  119 us
    pallas_call x1, Pallas kernels, shards(): pl.pallas_call(hand_over, out_shape=[jax.ShapeDtypeStruct(o.shape, o.dtyp...  2.58 us

profile of v6, /device:TPU:33, one launch (start us, length us, event | category | flops | bytes accessed | tf_op | source)
XLA Modules:
  0.0 122.5 jit_solution(7820575841115967545)
XLA Ops:
  0.6 119.3 %shard_map.147 = (bf16[128,5120]{1,0:T(8,128)(2,1)}, bf16[160,512]{1,0:T(8,128)(2,1)}, bf16[10,512]{1,0:T(8,128)(2,1)}, bf16[10,512]{1,0:T(8,128)(2,1)}) custom-call(bf16[128,5120]{1,0:T(8,128)(2,1)} %x_hbm.1, bf16[128,2560]{1,0:T(8,128)(2,1)} %q_hbm.1, bf16[128,512]{1,0:T(8,128)(2,1)} %k_hbm.1, bf16[128,2560]{1,0:T(8,128)(2,1)} %g_hbm.1, f32[1,128]{1,0:T(1,128)} %bitcast.5, ...), custom_call_target="tpu_custom_call" | custom-call | tf_op jit(solution)/shard_map/pallas_call | solution.py:792
  120.0 2.6 %shard_map.148 = (bf16[128,5120]{1,0:T(8,128)(2,1)}, bf16[160,512]{1,0:T(8,128)(2,1)}, bf16[10,512]{1,0:T(8,128)(2,1)}, bf16[10,512]{1,0:T(8,128)(2,1)}) custom-call(bf16[128,5120]{1,0:T(8,128)(2,1)} %get-tuple-element.8.ig_in, bf16[160,512]{1,0:T(8,128)(2,1)} %get-tuple-element.9.np_in, bf16[10,512]{1,0:T(8,128)(2,1)} %get-tuple-element.10.nf_in, ...), custom_call_target="tpu_custom_call" | custom-call | tf_op jit(solution)/shard_map/pallas_call | solution.py:889
